TPU v7x, 32 devices: a whole 2x2x4 slice. The times are simulated.
32 devices in a mesh: hier: 8 (over z, x), row: 4 (over y, core).
Axes of the slice: x: 2, y: 2, z: 4, core: 2. Of those that a mesh axis runs over, the one named last changes fastest.
Arguments:
- state: bfloat16 [24, 2, 1024, 1024], P('hier', None, 'row'), may hold values from -6 to 6
- prev_slope: float32 [24, 2, 1024, 1024], P('hier', None, 'row'), may hold values from -6 to 6
- accumulated: float32 [24, 2, 1024, 1024], P('hier', None, 'row'), may hold values from -6 to 6
- hamiltonian: bfloat16 [2, 1024, 1024], P(None, 'row'), as said below
- couple_v: float32 [6, 1024], replicated, may hold values from -4 to 4
- coupling: float32 [2, 6], replicated, may hold values from 0.2 to 1
- damping: float32 [6], replicated, may hold values from 0.2 to 2
- occupation: int32 [24, 6], P('hier'), may hold values from 0 to 2, as said below
- parents: int32 [24, 6], P('hier'), may hold values from -1 to 23, as said below
- children: int32 [24, 6], P('hier'), may hold values from -1 to 22, as said below
Outputs:
- slope: float32 [24, 2, 1024, 1024], P('hier', None, 'row')
- accumulated_out: float32 [24, 2, 1024, 1024], P('hier', None, 'row')
Inputs may be any that keep to these rules, and one draw needn't show every extreme that they name: `occupation`: row s is the index of the operator in slot s. The rows are the 24 indices of smallest total among all indices of 6 entries with total at most 4, taken by total and then lexicographically; the all-zero index stands in the last slot, the others in a slot order drawn from the seed; the set is closed under lowering one entry. `parents`: entry (s, k) is the slot whose index equals slot s's index with entry k lowered by one, or -1 where entry k of slot s is 0. `children`: entry (s, k) is the slot whose index equals slot s's index with entry k raised by one, or -1 where that index is not among the 24. `hamiltonian`: Hermitian: the real part is symmetric, the imaginary part antisymmetric.
All inputs are finite; a program needn't handle non-finite values.
Results may differ from a plain program's by a relative error of at most 0.0029.
Values may be sent and summed in bfloat16 or wider, within the bound.
No kernel may reach another device: no remote copies, remote signals or barrier semaphores. Data moves between devices by JAX's collectives and lax.ppermute only.
A program may use at most 320 MiB of HBM per device.

v0:
```python
import jax
import jax.numpy as jnp
from jax import lax
from jax.sharding import PartitionSpec as P

step_size = 0.5


def complex_einsum(form, left_real, left_imag, right_real, right_imag):
    real_part = jnp.einsum(
        form, left_real, right_real, preferred_element_type=jnp.float32
    ) - jnp.einsum(form, left_imag, right_imag, preferred_element_type=jnp.float32)
    imag_part = jnp.einsum(
        form, left_real, right_imag, preferred_element_type=jnp.float32
    ) + jnp.einsum(form, left_imag, right_real, preferred_element_type=jnp.float32)
    return jnp.stack([real_part, imag_part], axis=1)


def shards(
    state,
    prev_slope,
    accumulated,
    hamiltonian,
    couple_v,
    coupling,
    damping,
    occupation,
    parents,
    children,
):
    section = (state.astype(jnp.float32) + 0.5 * step_size * prev_slope).astype(jnp.bfloat16)
    local_rows = section.shape[2]
    modes = occupation.shape[1]
    whole_h = lax.all_gather(hamiltonian, "row", axis=1, tiled=True)
    right_side = complex_einsum("krc,cn->krn", section[:, 0], section[:, 1], whole_h[0], whole_h[1])
    columns = lax.all_to_all(section, "row", split_axis=3, concat_axis=2, tiled=True)
    dag_real = jnp.swapaxes(columns[:, 0], 1, 2)
    dag_imag = -jnp.swapaxes(columns[:, 1], 1, 2)
    product = complex_einsum("krc,cn->krn", dag_real, dag_imag, whole_h[0], whole_h[1])
    returned = lax.all_to_all(product, "row", split_axis=3, concat_axis=2, tiled=True)
    left_side = jnp.stack(
        [jnp.swapaxes(returned[:, 0], 1, 2), -jnp.swapaxes(returned[:, 1], 1, 2)], axis=1
    )
    offset = lax.axis_index("row") * local_rows
    vrows = lax.dynamic_slice_in_dim(couple_v, offset, local_rows, 1)
    diff = vrows[:, :, None] - couple_v[:, None, :]
    total = vrows[:, :, None] + couple_v[:, None, :]
    counts = occupation.astype(jnp.float32)
    targets = jnp.concatenate([children, parents], axis=1)
    piece = lax.all_gather(section, "hier", axis=0, tiled=True)
    slots = jnp.arange(piece.shape[0], dtype=jnp.int32)
    picks = (targets[:, :, None] == slots[None, None, :]).astype(jnp.bfloat16)
    chosen = jnp.einsum("kmc,cxrn->kmxrn", picks, piece, preferred_element_type=jnp.float32)
    picked = chosen.astype(jnp.bfloat16)
    upper = picked[:, :modes].astype(jnp.float32)
    lower = picked[:, modes:].astype(jnp.float32) * counts[:, :, None, None, None]
    g_real = coupling[0][:, None, None] * diff
    g_imag = coupling[1][:, None, None] * total
    add_real = jnp.sum(
        diff[None] * upper[:, :, 1] + g_real[None] * lower[:, :, 1] + g_imag[None] * lower[:, :, 0],
        axis=1,
    )
    add_imag = jnp.sum(
        -diff[None] * upper[:, :, 0]
        - g_real[None] * lower[:, :, 0]
        + g_imag[None] * lower[:, :, 1],
        axis=1,
    )
    coupled = jnp.stack([add_real, add_imag], axis=1)
    decay = jnp.sum(counts * damping[None, :], axis=1)
    commuted = left_side - right_side
    rotated = jnp.stack([commuted[:, 1], -commuted[:, 0]], axis=1)
    slope = rotated - decay[:, None, None, None] * section.astype(jnp.float32) + coupled
    return (slope, accumulated + step_size / 3.0 * slope)


def solution(mesh):
    return jax.shard_map(
        shards,
        mesh=mesh,
        in_specs=(
            P("hier", None, "row", None),
            P("hier", None, "row", None),
            P("hier", None, "row", None),
            P(None, "row", None),
            P(),
            P(),
            P(),
            P("hier", None),
            P("hier", None),
            P("hier", None),
        ),
        out_specs=(P("hier", None, "row", None), P("hier", None, "row", None)),
        check_vma=False,
    )
```

profile of v0, /device:TPU:0, one launch (start us, length us, event | category | flops | bytes accessed | tf_op | source)
XLA Modules:
  0.0 775.2 jit_solution(13469059892503589708)
XLA Ops:
  7.2 0.0 all-gather.3.cloned.1.call-start
  7.2 0.7 all-gather.3.cloned.1.call-update
  7.9 0.0 all-gather.5.cloned.1.call-start
  7.9 6.7 fusion.12
  14.6 0.0 all-gather.5.cloned.1.call-update
  14.6 1.9 copy-done
  16.5 5.6 copy.38
  22.1 56.7 %all_to_all.36 = bf16[3,2,256,1024]{2,1,0,3:T(2,128)(2,1)S(1)} all-to-all(bf16[3,2,256,1024]{2,1,0,3:T(2,128)(2,1)} %copy.38), channel_id=1, replica_groups=mesh['hier'=8,'row'=4] {'row'}, dimensions={3} | all-to-all | bytes 6291456 | tf_op jit(solution)/shard_map/all_to_all | solution.py:36
  78.9 4.1 copy.68
  83.0 6.1 all_to_all.29
  89.1 0.0 all-gather.3.cloned.1.call-done
  89.1 0.0 copy-start.3
  89.1 0.0 copy-start.11
  89.1 4.0 fusion.15
  93.1 0.0 copy-done.3
  93.1 0.2 copy-done.11
  93.3 1.8 fusion.16
  95.1 1.8 add_bitcast_fusion.1
  96.9 1.8 subtract_bitcast_fusion.1
  98.7 3.3 pad_maximum_fusion
  102.0 10.2 %copy.40 = f32[3,2,256,1024]{2,1,0,3:T(2,128)} copy(f32[3,2,256,1024]{3,2,0,1:T(8,128)} %pad_maximum_fusion) | data formatting | bytes 12582912 | tf_op jit(solution)/shard_map/stack | solution.py:16
  112.3 0.0 copy-start.5
  112.3 0.0 copy-start.4
  112.3 0.0 copy-start.7
  112.3 0.0 copy-start.8
  112.3 0.0 copy-start.10
  112.3 0.0 copy-start.9
  112.3 5.9 all-to-all-start.1
  118.3 0.0 copy-done.5
  118.3 0.0 copy-done.4
  118.3 0.1 copy.42
  118.4 0.0 copy-done.7
  118.5 0.0 copy-done.8
  118.5 0.1 pad_add_fusion
  118.5 0.0 copy-done.10
  118.5 0.6 multiply_reduce_fusion
  119.2 0.0 copy-done.9
  119.2 0.0 copy-start.12
  119.2 11.9 %subtract_negate_fusion = (f32[6,256,1024]{2,0,1:T(8,128)}, f32[6,256,1024]{2,0,1:T(8,128)}, f32[6,256,1024]{2,0,1:T(8,128)}, f32[6,256,1024]{2,0,1:T(8,128)}) fusion(f32[6,1024]{1,0:T(8,128)S(1)} %copy-done.4, f32[6,256]{0,1:T(8,128)S(1)} %copy.42, f32[6]{0:T(128)S(1)} %get-tuple-element.21, f32[6]{0:T(128)S(1)} %get-tuple-element.20), kind=kLoop, calls=%fused_computation.18 | loop fusion | flops 7864320 | bytes 25196592 | tf_op jit(solution)/shard_map/neg | solution.py:64
  131.1 0.0 copy-done.12
  131.1 1.8 fusion.17
  132.9 1.8 fusion.18
  134.7 3.4 add_bitcast_fusion
  138.1 3.4 subtract_bitcast_fusion
  141.6 47.4 %all-to-all-done.1 = f32[3,2,256,1024]{2,1,0,3:T(2,128)} async-done(((f32[3,2,256,1024]{2,1,0,3:T(2,128)}), f32[3,2,256,1024]{2,1,0,3:T(2,128)}, u32[]{:S(2)}, u32[]{:S(2)}) %all-to-all-start.1) | async-done | bytes 6291488 | tf_op jit(solution)/shard_map/all_to_all | solution.py:40
  188.9 9.5 %copy.67 = f32[3,2,256,4,256]{2,3,4,0,1:T(4,128)} copy(f32[3,2,256,4,256]{2,1,0,4,3:T(2,128)} %bitcast.14) | data formatting | bytes 12582912 | tf_op jit(solution)/shard_map/all_to_all | solution.py:40
  198.5 8.3 %all_to_all.33 = f32[3,2,1024,256]{2,3,0,1:T(8,128)} reshape(f32[3,2,4,256,256]{3,2,4,0,1:T(4,128)} %bitcast.117) | data formatting | bytes 12582912 | tf_op jit(solution)/shard_map/all_to_all | solution.py:40
  206.8 0.0 copy-start.1
  206.8 0.0 copy-start.2
  206.8 3.7 slice_bitcast_fusion.4
  210.5 0.1 copy-done.1
  210.5 1.0 copy-done.2
  211.5 1.9 maximum_subtract_fusion
  213.4 3.4 fusion.25
  216.8 326.7 %all-gather.5.cloned.1.call-done = bf16[24,2,256,1024]{3,2,0,1:T(8,128)(2,1)} async-done(((bf16[3,2,256,1024]{3,2,0,1:T(8,128)(2,1)}), bf16[24,2,256,1024]{3,2,0,1:T(8,128)(2,1)}) %all-gather.5.cloned.1.call-update) | async-done | bytes 25165840 | tf_op jit(solution)/shard_map/all_gather | solution.py:50
  543.5 98.1 %convolution_convert_fusion = bf16[3,12,2,256,1024]{4,1,3,2,0:T(8,128)(2,1)} fusion(bf16[24,2,256,1024]{3,2,0,1:T(8,128)(2,1)} %all-gather.5.cloned.1.call-done, s32[3,12]{1,0:T(4,128)S(1)} %pad_add_fusion), kind=kOutput, calls=%fused_computation.1 | convolution fusion | flops 924844928 | bytes 62914704 | tf_op jit(solution)/shard_map/kmc,cxrn->kmxrn/dot_general | solution.py:53
  641.6 27.3 %copy_convert_fusion = f32[3,6,2,256,1024]{4,1,3,0,2:T(8,128)} fusion(bf16[3,12,2,256,1024]{4,1,3,2,0:T(8,128)(2,1)} %convolution_convert_fusion), kind=kLoop, calls=%fused_computation.14 | loop fusion | flops 9437184 | bytes 62914560 | tf_op jit(solution)/shard_map/convert_element_type | solution.py:55
  668.9 37.2 %convert_multiply_fusion = f32[3,6,2,256,1024]{4,1,3,2,0:T(8,128)} fusion(bf16[3,12,2,256,1024]{4,1,3,2,0:T(8,128)(2,1)} %convolution_convert_fusion, f32[3,6]{1,0:T(4,128)S(1)} %convert_element_type.24), kind=kLoop, calls=%fused_computation | loop fusion | flops 18874368 | bytes 56623176 | tf_op jit(solution)/shard_map/mul | solution.py:56
  706.1 0.0 copy-start.6
  706.1 47.6 %fusion.7 = (f32[3,256,1024]{2,1,0:T(8,128)}, f32[3,256,1024]{2,1,0:T(8,128)}) fusion(f32[3,6,2,256,1024]{4,1,3,0,2:T(8,128)} %copy_convert_fusion, f32[3,6,2,256,1024]{4,1,3,2,0:T(8,128)} %convert_multiply_fusion, f32[6,256,1024]{2,0,1:T(8,128)} %get-tuple-element.17, f32[6,256,1024]{2,0,1:T(8,128)} %get-tuple-element.18, ...), kind=kLoop, calls=%fused_computation.13 | loop fusion | flops 55050240 | bytes 106954752 | tf_op jit(solution)/shard_map/reduce_sum | solution.py:59
  753.7 0.0 copy-done.6
  753.7 7.8 %copy_add_fusion = (f32[3,2,256,1024]{3,2,0,1:T(8,128)S(1)}, f32[3,2,256,1024]{3,2,0,1:T(8,128)S(1)}) fusion(f32[3,2,256,1024]{3,2,1,0:T(8,128)} %param.12, f32[3,1,256,1024]{3,2,0,1:T(8,128)} %bitcast.121, f32[3,1,256,1024]{3,2,0,1:T(8,128)} %bitcast.120, bf16[3,2,256,1024]{3,2,0,1:T(8,128)(2,1)S(1)} %copy-done, f32[3]{0:T(128)S(1)} %copy-done.6, ...), kind=kLoop, calls=%fused_computation.24 | loop fusion | flops 12582912 | bytes 34603020 | tf_op jit(solution)/shard_map/add | solution.py:74
  761.6 3.3 copy.47
  764.8 3.3 copy.48
  (4 shorter events, 0.0 us)
Async XLA Ops:
  7.2 81.9 %all-gather.3.cloned.1.call-start = ((), (), s32[]{:S(2)}) async-start(), calls=%async_computation.2 | async-start | bytes 5242880 | tf_op jit(solution)/shard_map/all_gather | solution.py:34
  7.9 535.6 %all-gather.5.cloned.1.call-start = ((), (), s32[]{:S(2)}) async-start(), calls=%async_computation.3 | async-start | bytes 28311552 | tf_op jit(solution)/shard_map/all_gather | solution.py:50
  14.6 1.9 copy-start
  89.1 4.0 copy-start.3
  89.1 4.2 copy-start.11
  112.3 6.0 copy-start.5
  112.3 6.0 copy-start.4
  112.3 6.2 copy-start.7
  112.3 6.2 copy-start.8
  112.3 6.3 copy-start.10
  112.3 6.9 copy-start.9
  112.3 76.6 %all-to-all-start.1 = ((f32[3,2,256,1024]{2,1,0,3:T(2,128)}), f32[3,2,256,1024]{2,1,0,3:T(2,128)}, u32[]{:S(2)}, u32[]{:S(2)}) async-start(f32[3,2,256,1024]{2,1,0,3:T(2,128)} %copy.40), calls=%async_computation.1 | async-start | bytes 12582912 | tf_op jit(solution)/shard_map/all_to_all | solution.py:40
  119.2 11.9 %copy-start.12 = (bf16[2,1024,1024]{2,1,0:T(8,128)(2,1)S(1)}, bf16[2,1024,1024]{2,1,0:T(8,128)(2,1)}, u32[]{:S(2)}) copy-start(bf16[2,1024,1024]{2,1,0:T(8,128)(2,1)} %all-gather.3.cloned.1.call-done) | copy-start | bytes 12582916
  206.8 3.7 copy-start.1
  206.8 4.7 copy-start.2
  706.1 47.6 %copy-start.6 = (f32[3]{0:T(128)S(1)}, f32[3]{0:T(128)}, u32[]{:S(2)}) copy-start(f32[3]{0:T(128)} %multiply_reduce_fusion) | copy-start | bytes 40
Sparse Core Ops, SparseCore 0:
  9.6 52.6 all-gather.2
  63.8 479.7 all-gather.4
where the time goes:
time: 784 us; the launch traced here: 775 us
  waiting for transfers between devices  375 us (48%)
  other arithmetic  152 us (19%)
  matrix products  118 us (15%)
  blocking collectives  56.7 us (7%)
  local copies, waits for them, and re-layouts  53.7 us (7%)
  between operations  14.4 us (2%)
    all_gather x1, waiting for transfers between devices, shards(): piece = lax.all_gather(section, 'hier', axis=0, tiled=True)  327 us
    dot_general x1, matrix products, shards(): jnp.einsum('kmc,cxrn->kmxrn', picks, piece, preferred_element_type=jnp.fl...  98.1 us
    all_to_all x1, blocking collectives, shards(): lax.all_to_all(section, 'row', split_axis=3, concat_axis=2, tiled=True)  56.7 us
    reduce_sum x1, other arithmetic, shards(): jnp.sum(diff[None] * upper[:, :, 1] + g_real[None] * lower[:, :, 1] + g_i...  47.6 us
    all_to_all x1, waiting for transfers between devices, shards(): lax.all_to_all(product, 'row', split_axis=3, concat_axis=2, tiled=True)  47.4 us
    mul x1, other arithmetic, shards(): picked[:, modes:].astype(jnp.float32) * counts[:, :, None, None, None]  37.2 us
    convert_element_type x1, other arithmetic, shards(): upper = picked[:, :modes].astype(jnp.float32)  27.3 us
    all_to_all x2, local copies, waits for them, and re-layouts, shards(): lax.all_to_all(product, 'row', split_axis=3, concat_axis=2, tiled=True)  17.8 us
  transfers between devices with their start and end apart: 3, of which 2 were waited for; matrix products, arithmetic and copies ran while one was open for 10% of the time, Pallas kernels for 0%

commit v1 on v0

v1 whole, which is shorter than its diff:
```python
import functools

import jax
import jax.numpy as jnp
import numpy as np
from jax import lax
from jax.experimental import pallas as pl
from jax.experimental.pallas import tpu as pltpu
from jax.sharding import PartitionSpec as P

step_size = 0.5
highest_total = 4
row_tile = 16
pieces = 2
MIB = 1024 * 1024
f32 = jnp.float32
bf16 = jnp.bfloat16


def index_rows(slots, modes):
    entries = [()]
    for _ in range(modes):
        entries = [
            entry + (level,)
            for entry in entries
            for level in range(highest_total + 1)
            if sum(entry) + level <= highest_total
        ]
    return sorted(entries, key=lambda entry: (sum(entry), entry))[:slots]


def coupled_to(rows):
    lookup = {entry: place for place, entry in enumerate(rows)}
    result = []
    for entry in rows:
        terms = []
        for mode, level in enumerate(entry):
            raised = entry[:mode] + (level + 1,) + entry[mode + 1 :]
            if raised in lookup:
                terms.append((lookup[raised], mode, True, 1))
            if level > 0:
                lowered = entry[:mode] + (level - 1,) + entry[mode + 1 :]
                terms.append((lookup[lowered], mode, False, level))
        result.append(terms)
    return result


def smaller_class(rows):
    classes = [[c for c, entry in enumerate(rows) if sum(entry) % 2 == rest] for rest in (0, 1)]
    return min(classes, key=len)


def params(megabytes):
    return pltpu.CompilerParams(vmem_limit_bytes=megabytes * MIB)


def whole():
    return pl.BlockSpec(memory_space=pltpu.VMEM)


def scalars():
    return pl.BlockSpec(memory_space=pltpu.SMEM)


def swap(array, axis, size, bit):
    return lax.ppermute(array, axis, [(i, i ^ bit) for i in range(size)])


def section_kernel(group, split, where, state, slope, section, *chunks):
    value = (state[...].astype(f32) + (0.5 * step_size) * slope[...]).astype(bf16)
    section[...] = value
    width = chunks[0].shape[-1]
    height = chunks[0].shape[-2]
    for b in range(group):
        columns = pl.ds(pl.multiple_of((where[0] ^ b) * width, 128), width)
        for p in range(split):
            chunks[b * split + p][...] = section[:, :, p * height : (p + 1) * height, columns]


def make_section(state, prev_slope, place, group, split):
    ops, parts, rows, columns = state.shape
    height, width = rows // split, columns // group
    block = pl.BlockSpec((1, 1, rows, columns), lambda a, x, _: (a, x, 0, 0))
    chunk = pl.BlockSpec((1, 1, height, width), lambda a, x, _: (a, x, 0, 0))
    count = group * split
    out = pl.pallas_call(
        functools.partial(section_kernel, group, split),
        grid_spec=pltpu.PrefetchScalarGridSpec(
            num_scalar_prefetch=1,
            grid=(ops, parts),
            in_specs=[block, block],
            out_specs=[block] + [chunk] * count,
        ),
        out_shape=[jax.ShapeDtypeStruct(state.shape, bf16)]
        + [jax.ShapeDtypeStruct((ops, parts, height, width), bf16)] * count,
        compiler_params=params(24),
        cost_estimate=pl.CostEstimate(
            flops=2 * state.size, bytes_accessed=10 * state.size, transcendentals=0
        ),
        name="section",
    )(place, state, prev_slope)
    return out[0], [[out[1 + b * split + p] for b in range(group)] for p in range(split)]


def fill_factors(vrows, vcols, coupling, factors):
    modes = vrows.shape[0]
    for k in range(modes):
        first = vrows[k]
        second = vcols[k : k + 1, :]
        diff = first - second
        factors[k] = diff
        factors[modes + k] = coupling[0, k] * diff
        factors[2 * modes + k] = coupling[1, k] * (first + second)


def add_terms(terms, places, held, factors, modes, rows, real, imag):
    for other, mode, child, count in terms:
        place = places[other]
        x_real = held[place, 0, rows, :].astype(f32)
        x_imag = held[place, 1, rows, :].astype(f32)
        if child:
            diff = factors[mode, rows, :]
            real = real + diff * x_imag
            imag = imag - diff * x_real
        else:
            first = factors[modes + mode, rows, :]
            second = factors[2 * modes + mode, rows, :]
            if count != 1:
                first, second = count * first, count * second
            real = real + (first * x_imag + second * x_real)
            imag = imag + (second * x_imag - first * x_real)
    return real, imag


def load_held(chunks, held):
    ops = chunks[0].shape[0]
    for b, chunk in enumerate(chunks):
        held[b * ops : (b + 1) * ops] = chunk[...]
    held[len(chunks) * ops] = jnp.zeros(held.shape[1:], bf16)


def partial_kernel(links, sides, group, places, coupling, vrows, vcols, *refs):
    chunks, out, held, factors = refs[:group], refs[group], refs[group + 1], refs[group + 2]
    modes = vrows.shape[0]
    height, width = held.shape[2:]
    empty = group * chunks[0].shape[0]
    fill_factors(vrows, vcols, coupling, factors)
    load_held(chunks, held)
    for u, c in enumerate(sides):

        @pl.when(places[c] < empty)
        def _():
            out[u] = held[places[c]]

        @pl.when(places[c] == empty)
        def _():
            @pl.loop(0, height // row_tile)
            def _(i):
                rows = pl.ds(pl.multiple_of(i * row_tile, row_tile), row_tile)
                zero = jnp.zeros((row_tile, width), f32)
                real, imag = add_terms(links[c], places, held, factors, modes, rows, zero, zero)
                out[u, 0, rows, :] = real.astype(bf16)
                out[u, 1, rows, :] = imag.astype(bf16)


def coupled_kernel(links, sides, group, places, coupling, vrows, vcols, *refs):
    chunks, received, outs = refs[:group], refs[group], refs[group + 1 : 2 * group + 1]
    held, done, factors, spots = refs[2 * group + 1 :]
    modes = vrows.shape[0]
    height, width = held.shape[2:]
    ops = chunks[0].shape[0]
    empty = group * ops
    fill_factors(vrows, vcols, coupling, factors)
    load_held(chunks, held)
    held[empty + 1 :] = received[...]
    for c in range(len(links)):
        spots[c] = places[c]
    for u, c in enumerate(sides):
        spots[c] = jnp.where(places[c] == empty, empty + 1 + u, places[c])
    for c in range(len(links)):

        @pl.when(places[c] < empty)
        def _():
            @pl.loop(0, height // row_tile)
            def _(i):
                rows = pl.ds(pl.multiple_of(i * row_tile, row_tile), row_tile)
                if c in sides:
                    u = empty + 1 + sides.index(c)
                    real, imag = held[u, 0, rows, :].astype(f32), held[u, 1, rows, :].astype(f32)
                else:
                    real = imag = jnp.zeros((row_tile, width), f32)
                real, imag = add_terms(links[c], spots, held, factors, modes, rows, real, imag)
                done[places[c], 0, rows, :] = real.astype(bf16)
                done[places[c], 1, rows, :] = imag.astype(bf16)

    for b, out in enumerate(outs):
        out[...] = done[b * ops : (b + 1) * ops]


def coupling_scratch(entries, height, width, modes):
    return [pltpu.VMEM((entries, 2, height, width), bf16)], [pltpu.VMEM((3 * modes, height, width), f32)]


def make_partial(chunks, places, coupling, vrows, vcols, links, sides):
    group = len(chunks)
    ops, _, height, width = chunks[0].shape
    held, factors = coupling_scratch(group * ops + 1, height, width, vrows.shape[0])
    size = height * width
    return pl.pallas_call(
        functools.partial(partial_kernel, links, sides, group),
        in_specs=[scalars(), scalars()] + [whole()] * (2 + group),
        out_specs=whole(),
        out_shape=jax.ShapeDtypeStruct((len(sides), 2, height, width), bf16),
        scratch_shapes=held + factors,
        compiler_params=params(32),
        cost_estimate=pl.CostEstimate(
            flops=40 * len(sides) * size,
            bytes_accessed=4 * size * (group * ops + len(sides)),
            transcendentals=0,
        ),
        name="partial_sums",
    )(places, coupling, vrows, vcols, *chunks)


def make_coupled(chunks, received, places, coupling, vrows, vcols, links, sides):
    group = len(chunks)
    ops, _, height, width = chunks[0].shape
    held, factors = coupling_scratch(group * ops + 1 + len(sides), height, width, vrows.shape[0])
    size = height * width
    return pl.pallas_call(
        functools.partial(coupled_kernel, links, sides, group),
        in_specs=[scalars(), scalars()] + [whole()] * (3 + group),
        out_specs=[whole()] * group,
        out_shape=[jax.ShapeDtypeStruct(chunks[0].shape, bf16)] * group,
        scratch_shapes=held
        + [pltpu.VMEM((group * ops, 2, height, width), bf16)]
        + factors
        + [pltpu.SMEM((len(links),), jnp.int32)],
        compiler_params=params(32),
        cost_estimate=pl.CostEstimate(
            flops=40 * group * ops * size,
            bytes_accessed=4 * size * (2 * group * ops + len(sides)),
            transcendentals=0,
        ),
        name="coupling_sums",
    )(places, coupling, vrows, vcols, *chunks, received)


def product_kernel(count, where, decay, h_own, s_own, *refs):
    s_parts, h_parts, out = refs[:count], refs[count : 2 * count], refs[2 * count]
    s_all, h_all = refs[2 * count + 1 :]
    a = pl.program_id(1)
    height = h_own.shape[1]

    def place(b):
        return pl.ds(pl.multiple_of((where[0] ^ b) * height, row_tile), height)

    @pl.when(a == 0)
    def _():
        for b in range(count):
            h_all[:, place(b), :] = h_parts[b][...]

    for b in range(count):
        s_all[:, place(b), :] = s_parts[b][0]

    def dot(left, right):
        return jnp.dot(left, right, preferred_element_type=f32)

    h_real, h_imag = h_own[0], h_own[1]
    s_real, s_imag = s_own[a, 0], s_own[a, 1]
    lost = decay[a]
    imag = dot(h_real, s_all[1]) + dot(h_imag, s_all[0])
    imag = imag - dot(s_real, h_all[1]) - dot(s_imag, h_all[0])
    out[0, 0] = imag - lost * s_parts[0][0, 0].astype(f32)
    real = dot(h_real, s_all[0]) - dot(h_imag, s_all[1])
    real = real - dot(s_real, h_all[0]) + dot(s_imag, h_all[1])
    out[0, 1] = -real - lost * s_parts[0][0, 1].astype(f32)


def make_product(s_parts, h_parts, place, decay):
    ops, _, rows, columns = s_parts[0].shape
    count = len(s_parts)
    tile = min(columns, 256)
    return pl.pallas_call(
        functools.partial(product_kernel, count),
        grid=(columns // tile, ops),
        in_specs=[
            scalars(),
            scalars(),
            pl.BlockSpec((2, rows, columns), lambda j, a: (0, 0, 0)),
            pl.BlockSpec((ops, 2, rows, columns), lambda j, a: (0, 0, 0, 0)),
        ]
        + [pl.BlockSpec((1, 2, rows, tile), lambda j, a: (a, 0, 0, j))] * count
        + [pl.BlockSpec((2, rows, tile), lambda j, a: (0, 0, j))] * count,
        out_specs=pl.BlockSpec((1, 2, rows, tile), lambda j, a: (a, 0, 0, j)),
        out_shape=jax.ShapeDtypeStruct((ops, 2, rows, columns), f32),
        scratch_shapes=[pltpu.VMEM((2, count * rows, tile), bf16)] * 2,
        compiler_params=params(32),
        cost_estimate=pl.CostEstimate(
            flops=16 * ops * rows * columns * columns,
            bytes_accessed=4 * count * (ops + 1) * rows * columns + 8 * ops * rows * columns,
            transcendentals=0,
        ),
        name="products",
    )(place, decay, h_parts[0], s_parts[0], *s_parts, *h_parts)


def final_kernel(group, split, where, product, accumulated, *refs):
    sums, slope, total = refs[: group * split], refs[group * split], refs[group * split + 1]
    b, a = pl.program_id(0), pl.program_id(1)
    height = sums[0].shape[2]
    for i in range(group):

        @pl.when(b == i)
        def _():
            for p in range(split):
                rows = slice(p * height, (p + 1) * height)
                value = product[0, :, rows, :] + sums[i * split + p][a].astype(f32)
                slope[0, :, rows, :] = value
                total[0, :, rows, :] = accumulated[0, :, rows, :] + (step_size / 3.0) * value


def make_final(product, accumulated, sums, place):
    ops, parts, rows, columns = product.shape
    split, group = len(sums), len(sums[0])
    width = columns // group
    block = pl.BlockSpec((1, parts, rows, width), lambda b, a, g: (a, 0, 0, g[0] ^ b))
    held = pl.BlockSpec(sums[0][0].shape, lambda b, a, g: (0, 0, 0, 0))
    return pl.pallas_call(
        functools.partial(final_kernel, group, split),
        grid_spec=pltpu.PrefetchScalarGridSpec(
            num_scalar_prefetch=1,
            grid=(group, ops),
            in_specs=[block, block] + [held] * (group * split),
            out_specs=[block, block],
        ),
        out_shape=[jax.ShapeDtypeStruct(product.shape, f32)] * 2,
        compiler_params=params(24),
        cost_estimate=pl.CostEstimate(
            flops=4 * product.size, bytes_accessed=18 * product.size, transcendentals=0
        ),
        name="outputs",
    )(place, product, accumulated, *[sums[p][b] for b in range(group) for p in range(split)])


def shards(
    hier,
    row,
    state,
    prev_slope,
    accumulated,
    hamiltonian,
    couple_v,
    coupling,
    damping,
    occupation,
    parents,
    children,
):
    ops, _, rows, columns = state.shape
    modes = occupation.shape[1]
    group = hier // 2
    width = columns // group
    split = pieces
    height = rows // split
    table = index_rows(hier * ops, modes)
    links, sides = coupled_to(table), smaller_class(table)

    hier_at, row_at = lax.axis_index("hier"), lax.axis_index("row")
    own = hier_at % group
    own_place, row_place = own.reshape(1).astype(jnp.int32), row_at.reshape(1).astype(jnp.int32)

    def gather_rows(array):
        parts = {0: array}
        bit = row // 2
        while bit:
            for mask in list(parts):
                parts[mask ^ bit] = swap(parts[mask], "row", row, bit)
            bit //= 2
        return [parts[b] for b in range(row)]

    h_parts = gather_rows(hamiltonian)
    section, chunks = make_section(state, prev_slope, own_place, group, split)

    everyone = lax.all_gather(occupation, "hier", axis=0, tiled=True)
    known = jnp.asarray(np.array(table, np.int32))
    same = jnp.all(everyone[:, None, :] == known[None, :, :], axis=2)
    slot = jnp.sum(jnp.where(same, jnp.arange(hier * ops, dtype=jnp.int32)[:, None], 0), axis=0)
    device = slot // ops
    places = jnp.where(
        device // group == hier_at // group,
        ((device % group) ^ own) * ops + slot % ops,
        group * ops,
    ).astype(jnp.int32)
    vrows = lax.dynamic_slice_in_dim(couple_v, row_at * rows, rows, 1)[:, :, None]
    vcols = lax.dynamic_slice_in_dim(couple_v, own * width, width, 1)
    decay = jnp.sum(occupation.astype(f32) * damping[None, :], axis=1)

    sums = []
    for p in range(split):
        here = vrows[:, p * height : (p + 1) * height]
        got = [chunks[p][0]] + [swap(chunks[p][b], "hier", hier, b) for b in range(1, group)]
        sent = make_partial(got, places, coupling, here, vcols, links, sides)
        received = swap(sent, "hier", hier, group)
        done = make_coupled(got, received, places, coupling, here, vcols, links, sides)
        sums.append([done[0]] + [swap(done[b], "hier", hier, b) for b in range(1, group)])

    s_parts = gather_rows(section)
    product = make_product(s_parts, h_parts, row_place, decay)
    slope, total = make_final(product, accumulated, sums, own_place)
    return slope, total


def solution(mesh):
    return jax.shard_map(
        functools.partial(shards, mesh.shape["hier"], mesh.shape["row"]),
        mesh=mesh,
        in_specs=(
            P("hier", None, "row", None),
            P("hier", None, "row", None),
            P("hier", None, "row", None),
            P(None, "row", None),
            P(),
            P(),
            P(),
            P("hier", None),
            P("hier", None),
            P("hier", None),
        ),
        out_specs=(P("hier", None, "row", None), P("hier", None, "row", None)),
        check_vma=False,
    )
```

time: 784 us -> 250 us (0.32); the launches traced: 775 us -> 249 us
  waiting for transfers between devices: 375 us -> 128 us
  other arithmetic: 152 us -> 2.79 us
  matrix products: 118 us -> 0 us
  Pallas kernels: 0 us -> 44.1 us
  local copies, waits for them, and re-layouts: 53.7 us -> 13.8 us
  blocking collectives: 56.7 us -> 38.4 us
  starting transfers between devices: 6.02 us -> 21.8 us
  between operations: 14.4 us -> 0.82 us
    all_gather x2 -> x0, waiting for transfers between devices: 327 us -> none  [the longest x1 327 us: shards(): piece = lax.all_gather(section, 'hier', axis=0, tiled=True)]
    ppermute x0 -> x20, waiting for transfers between devices: none -> 128 us  [swap(): return lax.ppermute(array, axis, [(i, i ^ bit) for i in range(size)])]
    dot_general x9 -> x0, matrix products: 118 us -> none  [the longest x1 98.1 us: shards(): jnp.einsum('kmc,cxrn->kmxrn', picks, piece, preferred_element_type=jnp.fl...]
    all_to_all x1 -> x0, blocking collectives: 56.7 us -> none  [shards(): lax.all_to_all(section, 'row', split_axis=3, concat_axis=2, tiled=True)]
    all_to_all x1 -> x0, waiting for transfers between devices: 47.4 us -> none  [shards(): lax.all_to_all(product, 'row', split_axis=3, concat_axis=2, tiled=True)]
    reduce_sum x2, other arithmetic: 48.3 us -> 1.33 us  [the longest x1 0.8 us: shards(): decay = jnp.sum(occupation.astype(f32) * damping[None, :], axis=1)]
    pallas_call x0 -> x7, Pallas kernels: none -> 44.1 us  [the longest x1 21 us: make_product(): pl.pallas_call(functools.partial(product_kernel, count), grid=(columns //...]
    all_gather x0 -> x1, blocking collectives: none -> 38.4 us  [shards(): everyone = lax.all_gather(occupation, 'hier', axis=0, tiled=True)]
  transfers between devices with their start and end apart: 3 -> 20, of which waited for: 2 -> 8; matrix products, arithmetic and copies ran while one was open for 10% -> 4% of each run, Pallas kernels for 0% -> 13%
where the time goes in v1:
time: 250 us; the launch traced here: 249 us
  waiting for transfers between devices  128 us (51%)
  Pallas kernels  44.1 us (18%)
  blocking collectives  38.4 us (15%)
  starting transfers between devices  21.8 us (9%)
  local copies, waits for them, and re-layouts  13.8 us (6%)
  other arithmetic  2.79 us (1%)
    ppermute x20, waiting for transfers between devices, swap(): return lax.ppermute(array, axis, [(i, i ^ bit) for i in range(size)])  128 us
    all_gather x1, blocking collectives, shards(): everyone = lax.all_gather(occupation, 'hier', axis=0, tiled=True)  38.4 us
    ppermute x20, starting transfers between devices, swap(): return lax.ppermute(array, axis, [(i, i ^ bit) for i in range(size)])  21.8 us
    pallas_call x1, Pallas kernels, make_product(): pl.pallas_call(functools.partial(product_kernel, count), grid=(columns //...  21 us
    unnamed x18, local copies, waits for them, and re-layouts  11.2 us
    pallas_call x1, Pallas kernels, make_final(): pl.pallas_call(functools.partial(final_kernel, group, split), grid_spec=p...  7.4 us
    pallas_call x2, Pallas kernels, make_coupled(): pl.pallas_call(functools.partial(coupled_kernel, links, sides, group), in...  6.94 us
    pallas_call x2, Pallas kernels, make_partial(): pl.pallas_call(functools.partial(partial_kernel, links, sides, group), in...  5.34 us
  transfers between devices with their start and end apart: 20, of which 8 were waited for; matrix products, arithmetic and copies ran while one was open for 4% of the time, Pallas kernels for 13%

profile of v1, /device:TPU:0, one launch (start us, length us, event | category | flops | bytes accessed | tf_op | source)
XLA Modules:
  0.0 249.4 jit_solution(5522054148709023338)
XLA Ops:
  0.6 0.0 copy-start.4
  0.6 0.0 copy-start.3
  0.7 0.0 copy-start
  0.7 2.8 %copy-done = f32[3,2,256,1024]{3,2,1,0:T(8,128)S(1)} copy-done((f32[3,2,256,1024]{3,2,1,0:T(8,128)S(1)}, f32[3,2,256,1024]{3,2,1,0:T(8,128)}, u32[]{:S(2)}) %copy-start) | copy-done | bytes 6291480
  3.5 1.9 copy-done.2
  5.3 3.4 %section.1 = (bf16[3,2,256,1024]{3,2,1,0:T(8,128)(2,1)}, bf16[3,2,128,256]{3,2,1,0:T(8,128)(2,1)S(1)}, bf16[3,2,128,256]{3,2,1,0:T(8,128)(2,1)S(1)}, bf16[3,2,12...) custom-call(s32[1]{0:T(128)} %bitcast.where, ...), custom_call_target="tpu_custom_call" | custom-call | flops 3145728 | bytes 15728640 | tf_op jit(solution)/shard_map/section/pallas_call | solution.py:86
  8.8 3.0 %collective-permute-start.1 = (bf16[3,2,256,1024]{3,2,1,0:T(8,128)(2,1)}, bf16[3,2,256,1024]{3,2,1,0:T(8,128)(2,1)}, u32[]{:S(2)}, u32[]{:S(2)}) collective-permute-start(bf16[3,2,256,1024]{3,2,1,0:T(8,128)(2,1)} %get-tuple-element.19.s_own.refs_0_), channel_id=1, source_target_pairs={{0,2},{1,3},{2,0},{3,1},{4,6},{5,7},{6,4},{7,5},{8,10},{9,11},{10,... | collective-permute-start | bytes 9437192 | tf_op jit(solution)/shard_map/ppermute | solution.py:66
  11.8 0.0 collective-permute-start
  11.8 68.4 %collective-permute-done.1.refs_2_ = bf16[3,2,256,1024]{3,2,1,0:T(8,128)(2,1)} collective-permute-done((bf16[3,2,256,1024]{3,2,1,0:T(8,128)(2,1)}, bf16[3,2,256,1024]{3,2,1,0:T(8,128)(2,1)}, u32[]{:S(2)}, u32[]{:S(2)}) %collective-permute-start.1) | collective-permute-done | bytes 3145760 | tf_op jit(solution)/shard_map/ppermute | solution.py:66
  80.2 0.0 collective-permute-start.2
  80.2 1.7 collective-permute-start.6
  81.9 1.6 collective-permute-start.7
  83.5 0.2 collective-permute-start.8
  83.7 1.4 constant_dynamic-slice_fusion
  85.0 38.4 %all-gather = s32[8,3,6]{2,1,0:T(4,128)} all-gather(s32[1,3,6]{2,1,0:T(4,128)S(1)} %bitcast.7), channel_id=1, replica_groups=mesh['hier'=8,'row'=4] {'hier'}, dimensions={0}, use_global_device_ids=true | all-gather | bytes 648 | tf_op jit(solution)/shard_map/all_gather | solution.py:385
  123.4 1.3 reshape.17
  124.8 1.4 copy.22
  126.1 1.3 fusion.3
  127.4 0.0 collective-permute-done.6.refs_1_
  127.4 0.0 collective-permute-start.10
  127.4 0.8 compare_reduce_fusion
  128.2 0.0 collective-permute-done.7.refs_2_
  128.2 1.6 collective-permute-start.4
  129.8 0.5 select_reduce_fusion
  130.3 0.2 copy.23.vrows
  130.5 0.0 collective-permute-done.8.refs_3_
  130.5 0.2 collective-permute-start.11
  130.7 0.7 compare_select_fusion.places
  131.4 2.9 %partial_sums.2 = bf16[6,2,128,256]{3,2,1,0:T(8,128)(2,1)} custom-call(s32[24]{0:T(128)S(1)} %compare_select_fusion.places, f32[2,6]{1,0:T(2,128)S(1)} %copy-done.3, f32[6,128,1]{2,1,0:T(8,128)S(1)} %copy.23.vrows, f32[6,256]{1,0:T(8,128)S(1)} %get-tuple-element.36.vcols, bf16[3,2,128,256]{3,2,1,0:T(8,128)(2,1)S(1)} %get-tuple-element.20.refs_0_, ...), custom_call_target="tpu_custom_call" | custom-call | flops 7864320 | bytes 2359296 | tf_op jit(solution)/shard_map/partial_sums/pallas_call | solution.py:209
  134.3 1.1 collective-permute-done.10.refs_1_
  135.4 1.0 collective-permute-start.9
  136.4 9.0 %collective-permute-done.11.refs_2_ = bf16[3,2,128,256]{3,2,1,0:T(8,128)(2,1)S(1)} collective-permute-done((bf16[3,2,128,256]{3,2,1,0:T(8,128)(2,1)S(1)}, bf16[3,2,128,256]{3,2,1,0:T(8,128)(2,1)S(1)}, u32[]{:S(2)}, u32[]{:S(2)}) %collective-permute-start.11) | collective-permute-done | bytes 393248 | tf_op jit(solution)/shard_map/ppermute | solution.py:66
  145.5 1.5 collective-permute-start.12
  147.0 0.8 copy.24.vrows
  147.8 13.4 %collective-permute-done.12.refs_3_ = bf16[3,2,128,256]{3,2,1,0:T(8,128)(2,1)} collective-permute-done((bf16[3,2,128,256]{3,2,1,0:T(8,128)(2,1)}, bf16[3,2,128,256]{3,2,1,0:T(8,128)(2,1)}, u32[]{:S(2)}, u32[]{:S(2)}) %collective-permute-start.12) | collective-permute-done | bytes 393248 | tf_op jit(solution)/shard_map/ppermute | solution.py:66
  161.2 2.5 partial_sums.3
  163.7 3.9 %collective-permute-start.13 = (bf16[6,2,128,256]{3,2,1,0:T(8,128)(2,1)S(1)}, bf16[6,2,128,256]{3,2,1,0:T(8,128)(2,1)S(1)}, u32[]{:S(2)}, u32[]{:S(2)}) collective-permute-start(bf16[6,2,128,256]{3,2,1,0:T(8,128)(2,1)S(1)} %partial_sums.3), channel_id=1, source_target_pairs={{0,16},{4,20},{8,24},{12,28},{16,0},{20,4},{24,8},{28,12},{1,17},{... | collective-permute-start | bytes 2359304 | tf_op jit(solution)/shard_map/ppermute | solution.py:66
  167.6 0.0 collective-permute-done.4.refs_6_
  167.6 0.0 collective-permute-start.3
  167.6 20.2 %collective-permute-done.9.refs_4_ = bf16[6,2,128,256]{3,2,1,0:T(8,128)(2,1)} collective-permute-done((bf16[6,2,128,256]{3,2,1,0:T(8,128)(2,1)}, bf16[6,2,128,256]{3,2,1,0:T(8,128)(2,1)}, u32[]{:S(2)}, u32[]{:S(2)}) %collective-permute-start.9) | collective-permute-done | bytes 786464 | tf_op jit(solution)/shard_map/ppermute | solution.py:66
  187.8 0.0 collective-permute-start.5
  187.8 3.5 %coupling_sums.2 = (bf16[3,2,128,256]{3,2,1,0:T(8,128)(2,1)S(1)}, bf16[3,2,128,256]{3,2,1,0:T(8,128)(2,1)S(1)}, bf16[3,2,128,256]{3,2,1,0:T(8,128)(2,1)S(1)}, bf16[3,2,128,256]{3,2,1,0:T(8,128)(2,1)S(1)}) custom-call(s32[24]{0:T(128)S(1)} %compare_select_fusion.places, f32[2,6]{1,0:T(2,128)S(1)} %copy-done.3, f32[6,128,1]{2,1,0:T(8,128)S(1)} %copy.23.vrows, ...), custom_call_target="tpu_custom_call" | custom-call | flops 15728640 | bytes 3932160 | tf_op jit(solution)/shard_map/coupling_sums/pallas_call | solution.py:230
  191.3 9.6 %collective-permute-done.13.refs_4_ = bf16[6,2,128,256]{3,2,1,0:T(8,128)(2,1)S(1)} collective-permute-done((bf16[6,2,128,256]{3,2,1,0:T(8,128)(2,1)S(1)}, bf16[6,2,128,256]{3,2,1,0:T(8,128)(2,1)S(1)}, u32[]{:S(2)}, u32[]{:S(2)}) %collective-permute-start.13) | collective-permute-done | bytes 786464 | tf_op jit(solution)/shard_map/ppermute | solution.py:66
  200.9 1.4 collective-permute-start.14
  202.3 0.8 multiply_reduce_fusion.decay
  203.1 3.5 %coupling_sums.3 = (bf16[3,2,128,256]{3,2,1,0:T(8,128)(2,1)S(1)}, bf16[3,2,128,256]{3,2,1,0:T(8,128)(2,1)S(1)}, bf16[3,2,128,256]{3,2,1,0:T(8,128)(2,1)S(1)}, bf16[3,2,128,256]{3,2,1,0:T(8,128)(2,1)S(1)}) custom-call(s32[24]{0:T(128)S(1)} %compare_select_fusion.places, f32[2,6]{1,0:T(2,128)S(1)} %copy-done.3, f32[6,128,1]{2,1,0:T(8,128)S(1)} %copy.24.vrows, ...), custom_call_target="tpu_custom_call" | custom-call | flops 15728640 | bytes 3932160 | tf_op jit(solution)/shard_map/coupling_sums/pallas_call | solution.py:230
  206.6 0.0 collective-permute-done.3.refs_5_
  206.6 0.1 collective-permute-start.16
  206.7 2.7 %collective-permute-done.14.refs_2_ = bf16[3,2,128,256]{3,2,1,0:T(8,128)(2,1)S(1)} collective-permute-done((bf16[3,2,128,256]{3,2,1,0:T(8,128)(2,1)S(1)}, bf16[3,2,128,256]{3,2,1,0:T(8,128)(2,1)S(1)}, u32[]{:S(2)}, u32[]{:S(2)}) %collective-permute-start.14) | collective-permute-done | bytes 393248 | tf_op jit(solution)/shard_map/ppermute | solution.py:66
  209.3 0.0 collective-permute-start.18
  209.3 0.0 collective-permute-done.5.refs_7_
  209.3 2.7 %collective-permute-start.15 = (bf16[3,2,128,256]{3,2,1,0:T(8,128)(2,1)S(1)}, bf16[3,2,128,256]{3,2,1,0:T(8,128)(2,1)S(1)}, u32[]{:S(2)}, u32[]{:S(2)}) collective-permute-start(bf16[3,2,128,256]{3,2,1,0:T(8,128)(2,1)S(1)} %get-tuple-element.31), channel_id=1, source_target_pairs={{0,4},{4,0},{8,12},{12,8},{16,20},{20,16},{24,28},{28,24},{1,5},{5... | collective-permute-start | bytes 1179656 | tf_op jit(solution)/shard_map/ppermute | solution.py:66
  212.0 0.0 collective-permute-done.refs_1_
  212.0 1.5 collective-permute-start.17
  213.6 0.0 collective-permute-done.2.refs_3_
  213.6 1.5 collective-permute-start.19
  215.0 21.0 %products.1.product = f32[3,2,256,1024]{3,2,1,0:T(8,128)} custom-call(s32[1]{0:T(128)} %bitcast.1.where, f32[3]{0:T(128)S(1)} %multiply_reduce_fusion.decay, bf16[2,256,1024]{2,1,0:T(8,128)(2,1)} %refs_4_.1, bf16[3,2,256,1024]{3,2,1,0:T(8,128)(2,1)} %get-tuple-element.19.s_own.refs_0_, bf16[3,2,256,1024]{3,2,1,0:T(8,128)(2,1)} %get-tuple-element.19.s_own.refs_0_, ...), custom_call_target="tpu_custom_call" | custom-call | flops 12884901888 | bytes 23068672 | tf_op jit(solution)/shard_map/products/pallas_call | solution.py:284
  236.0 0.0 collective-permute-done.16.refs_4_
  236.0 0.0 collective-permute-done.18.refs_6_
  236.1 0.0 collective-permute-done.15.refs_3_
  236.1 0.0 collective-permute-done.17.refs_5_
  236.1 3.1 %collective-permute-done.19.refs_7_ = bf16[3,2,128,256]{3,2,1,0:T(8,128)(2,1)S(1)} collective-permute-done((bf16[3,2,128,256]{3,2,1,0:T(8,128)(2,1)S(1)}, bf16[3,2,128,256]{3,2,1,0:T(8,128)(2,1)S(1)}, u32[]{:S(2)}, u32[]{:S(2)}) %collective-permute-start.19) | collective-permute-done | bytes 393248 | tf_op jit(solution)/shard_map/ppermute | solution.py:66
  239.2 2.8 %copy-done.1 = f32[3,2,256,1024]{3,2,1,0:T(8,128)S(1)} copy-done((f32[3,2,256,1024]{3,2,1,0:T(8,128)S(1)}, f32[3,2,256,1024]{3,2,1,0:T(8,128)}, u32[]{:S(2)}) %copy-start.1) | copy-done | bytes 6291480
  242.0 7.4 %outputs.1 = (f32[3,2,256,1024]{3,2,1,0:T(8,128)}, f32[3,2,256,1024]{3,2,1,0:T(8,128)}) custom-call(s32[1]{0:T(128)} %bitcast.where, f32[3,2,256,1024]{3,2,1,0:T(8,128)S(1)} %copy-done.1, f32[3,2,256,1024]{3,2,1,0:T(8,128)S(1)} %bitcast.6, bf16[3,2,128,256]{3,2,1,0:T(8,128)(2,1)S(1)} %get-tuple-element.24.refs_0_, ...), custom_call_target="tpu_custom_call" | custom-call | flops 6291456 | bytes 28311552 | tf_op jit(solution)/shard_map/outputs/pallas_call | solution.py:329
  (9 shorter events, 0.0 us)
Async XLA Ops:
  0.6 84.4 %copy-start.4 = (s32[3,6]{1,0:T(4,128)S(1)}, s32[3,6]{1,0:T(4,128)}, u32[]{:S(2)}) copy-start(s32[3,6]{1,0:T(4,128)} %param.18) | copy-start | bytes 220
  0.6 130.8 %copy-start.3 = (f32[2,6]{1,0:T(2,128)S(1)}, f32[2,6]{1,0:T(2,128)}, u32[]{:S(2)}) copy-start(f32[2,6]{1,0:T(2,128)} %coupling.7) | copy-start | bytes 148
  0.7 2.8 %copy-start = (f32[3,2,256,1024]{3,2,1,0:T(8,128)S(1)}, f32[3,2,256,1024]{3,2,1,0:T(8,128)}, u32[]{:S(2)}) copy-start(f32[3,2,256,1024]{3,2,1,0:T(8,128)} %slope.1) | copy-start | bytes 18874372
  3.5 1.9 copy-start.2
  8.8 71.4 %collective-permute-start.1 = (bf16[3,2,256,1024]{3,2,1,0:T(8,128)(2,1)}, bf16[3,2,256,1024]{3,2,1,0:T(8,128)(2,1)}, u32[]{:S(2)}, u32[]{:S(2)}) collective-permute-start(bf16[3,2,256,1024]{3,2,1,0:T(8,128)(2,1)} %get-tuple-element.19.s_own.refs_0_), channel_id=1, source_target_pairs={{0,2},{1,3},{2,0},{3,1},{4,6},{5,7},{6,4},{7,5},{8,10},{9,11},{10,... | collective-permute-start | bytes 9437192 | tf_op jit(solution)/shard_map/ppermute | solution.py:66
  11.8 200.3 %collective-permute-start = (bf16[3,2,256,1024]{3,2,1,0:T(8,128)(2,1)}, bf16[3,2,256,1024]{3,2,1,0:T(8,128)(2,1)}, u32[]{:S(2)}, u32[]{:S(2)}) collective-permute-start(bf16[3,2,256,1024]{3,2,1,0:T(8,128)(2,1)} %get-tuple-element.19.s_own.refs_0_), channel_id=1, source_target_pairs={{0,1},{1,0},{2,3},{3,2},{4,5},{5,4},{6,7},{7,6},{8,9},{9,8},{10,11... | collective-permute-start | bytes 9437192 | tf_op jit(solution)/shard_map/ppermute | solution.py:66
  80.2 133.4 %collective-permute-start.2 = (bf16[3,2,256,1024]{3,2,1,0:T(8,128)(2,1)}, bf16[3,2,256,1024]{3,2,1,0:T(8,128)(2,1)}, u32[]{:S(2)}, u32[]{:S(2)}) collective-permute-start(bf16[3,2,256,1024]{3,2,1,0:T(8,128)(2,1)} %collective-permute-done.1.refs_2_), channel_id=1, source_target_pairs={{0,1},{1,0},{2,3},{3,2},{4,5},{5,4},{6,7},{7,6},{8,9},{9,8},{10,11... | collective-permute-start | bytes 9437192 | tf_op jit(solution)/shard_map/ppermute | solution.py:66
  80.2 47.2 %collective-permute-start.6 = (bf16[3,2,128,256]{3,2,1,0:T(8,128)(2,1)S(1)}, bf16[3,2,128,256]{3,2,1,0:T(8,128)(2,1)S(1)}, u32[]{:S(2)}, u32[]{:S(2)}) collective-permute-start(bf16[3,2,128,256]{3,2,1,0:T(8,128)(2,1)S(1)} %get-tuple-element.21), channel_id=1, source_target_pairs={{0,4},{4,0},{8,12},{12,8},{16,20},{20,16},{24,28},{28,24},{1,5},{5... | collective-permute-start | bytes 1179656 | tf_op jit(solution)/shard_map/ppermute | solution.py:66
  81.9 46.3 %collective-permute-start.7 = (bf16[3,2,128,256]{3,2,1,0:T(8,128)(2,1)S(1)}, bf16[3,2,128,256]{3,2,1,0:T(8,128)(2,1)S(1)}, u32[]{:S(2)}, u32[]{:S(2)}) collective-permute-start(bf16[3,2,128,256]{3,2,1,0:T(8,128)(2,1)S(1)} %get-tuple-element.22), channel_id=1, source_target_pairs={{0,8},{4,12},{8,0},{12,4},{16,24},{20,28},{24,16},{28,20},{1,9},{5... | collective-permute-start | bytes 1179656 | tf_op jit(solution)/shard_map/ppermute | solution.py:66
  83.5 47.1 %collective-permute-start.8 = (bf16[3,2,128,256]{3,2,1,0:T(8,128)(2,1)S(1)}, bf16[3,2,128,256]{3,2,1,0:T(8,128)(2,1)S(1)}, u32[]{:S(2)}, u32[]{:S(2)}) collective-permute-start(bf16[3,2,128,256]{3,2,1,0:T(8,128)(2,1)S(1)} %get-tuple-element.23), channel_id=1, source_target_pairs={{0,12},{4,8},{8,4},{12,0},{16,28},{20,24},{24,20},{28,16},{1,13},{... | collective-permute-start | bytes 1179656 | tf_op jit(solution)/shard_map/ppermute | solution.py:66
  127.4 8.0 %collective-permute-start.10 = (bf16[3,2,128,256]{3,2,1,0:T(8,128)(2,1)}, bf16[3,2,128,256]{3,2,1,0:T(8,128)(2,1)S(1)}, u32[]{:S(2)}, u32[]{:S(2)}) collective-permute-start(bf16[3,2,128,256]{3,2,1,0:T(8,128)(2,1)} %get-tuple-element.26), channel_id=1, source_target_pairs={{0,4},{4,0},{8,12},{12,8},{16,20},{20,16},{24,28},{28,24},{1,5},{5... | collective-permute-start | bytes 1179656 | tf_op jit(solution)/shard_map/ppermute | solution.py:66
  128.2 39.3 %collective-permute-start.4 = (bf16[2,256,1024]{2,1,0:T(8,128)(2,1)}, bf16[2,256,1024]{2,1,0:T(8,128)(2,1)}, u32[]{:S(2)}, u32[]{:S(2)}) collective-permute-start(bf16[2,256,1024]{2,1,0:T(8,128)(2,1)} %refs_4_.1), channel_id=1, source_target_pairs={{0,2},{1,3},{2,0},{3,1},{4,6},{5,7},{6,4},{7,5},{8,10},{9,11},{10,... | collective-permute-start | bytes 3145736 | tf_op jit(solution)/shard_map/ppermute | solution.py:66
  130.5 14.9 %collective-permute-start.11 = (bf16[3,2,128,256]{3,2,1,0:T(8,128)(2,1)S(1)}, bf16[3,2,128,256]{3,2,1,0:T(8,128)(2,1)S(1)}, u32[]{:S(2)}, u32[]{:S(2)}) collective-permute-start(bf16[3,2,128,256]{3,2,1,0:T(8,128)(2,1)S(1)} %get-tuple-element.27), channel_id=1, source_target_pairs={{0,8},{4,12},{8,0},{12,4},{16,24},{20,28},{24,16},{28,20},{1,9},{5... | collective-permute-start | bytes 1179656 | tf_op jit(solution)/shard_map/ppermute | solution.py:66
  135.4 52.4 %collective-permute-start.9 = (bf16[6,2,128,256]{3,2,1,0:T(8,128)(2,1)}, bf16[6,2,128,256]{3,2,1,0:T(8,128)(2,1)}, u32[]{:S(2)}, u32[]{:S(2)}) collective-permute-start(bf16[6,2,128,256]{3,2,1,0:T(8,128)(2,1)} %partial_sums.2), channel_id=1, source_target_pairs={{0,16},{4,20},{8,24},{12,28},{16,0},{20,4},{24,8},{28,12},{1,17},{... | collective-permute-start | bytes 2359304 | tf_op jit(solution)/shard_map/ppermute | solution.py:66
  145.5 15.8 %collective-permute-start.12 = (bf16[3,2,128,256]{3,2,1,0:T(8,128)(2,1)}, bf16[3,2,128,256]{3,2,1,0:T(8,128)(2,1)}, u32[]{:S(2)}, u32[]{:S(2)}) collective-permute-start(bf16[3,2,128,256]{3,2,1,0:T(8,128)(2,1)} %get-tuple-element.28), channel_id=1, source_target_pairs={{0,12},{4,8},{8,4},{12,0},{16,28},{20,24},{24,20},{28,16},{1,13},{... | collective-permute-start | bytes 1179656 | tf_op jit(solution)/shard_map/ppermute | solution.py:66
  163.7 37.2 %collective-permute-start.13 = (bf16[6,2,128,256]{3,2,1,0:T(8,128)(2,1)S(1)}, bf16[6,2,128,256]{3,2,1,0:T(8,128)(2,1)S(1)}, u32[]{:S(2)}, u32[]{:S(2)}) collective-permute-start(bf16[6,2,128,256]{3,2,1,0:T(8,128)(2,1)S(1)} %partial_sums.3), channel_id=1, source_target_pairs={{0,16},{4,20},{8,24},{12,28},{16,0},{20,4},{24,8},{28,12},{1,17},{... | collective-permute-start | bytes 2359304 | tf_op jit(solution)/shard_map/ppermute | solution.py:66
  167.6 39.0 %collective-permute-start.3 = (bf16[2,256,1024]{2,1,0:T(8,128)(2,1)}, bf16[2,256,1024]{2,1,0:T(8,128)(2,1)S(1)}, u32[]{:S(2)}, u32[]{:S(2)}) collective-permute-start(bf16[2,256,1024]{2,1,0:T(8,128)(2,1)} %refs_4_.1), channel_id=1, source_target_pairs={{0,1},{1,0},{2,3},{3,2},{4,5},{5,4},{6,7},{7,6},{8,9},{9,8},{10,11... | collective-permute-start | bytes 3145736 | tf_op jit(solution)/shard_map/ppermute | solution.py:66
  187.8 21.6 %collective-permute-start.5 = (bf16[2,256,1024]{2,1,0:T(8,128)(2,1)}, bf16[2,256,1024]{2,1,0:T(8,128)(2,1)S(1)}, u32[]{:S(2)}, u32[]{:S(2)}) collective-permute-start(bf16[2,256,1024]{2,1,0:T(8,128)(2,1)} %collective-permute-done.4.refs_6_), channel_id=1, source_target_pairs={{0,1},{1,0},{2,3},{3,2},{4,5},{5,4},{6,7},{7,6},{8,9},{9,8},{10,11... | collective-permute-start | bytes 3145736 | tf_op jit(solution)/shard_map/ppermute | solution.py:66
  200.9 8.5 %collective-permute-start.14 = (bf16[3,2,128,256]{3,2,1,0:T(8,128)(2,1)S(1)}, bf16[3,2,128,256]{3,2,1,0:T(8,128)(2,1)S(1)}, u32[]{:S(2)}, u32[]{:S(2)}) collective-permute-start(bf16[3,2,128,256]{3,2,1,0:T(8,128)(2,1)S(1)} %get-tuple-element.30), channel_id=1, source_target_pairs={{0,4},{4,0},{8,12},{12,8},{16,20},{20,16},{24,28},{28,24},{1,5},{5... | collective-permute-start | bytes 1179656 | tf_op jit(solution)/shard_map/ppermute | solution.py:66
  203.1 36.1 %slice-start = ((s8[6291456]{0:T(1024)(128)(4,1)}), s8[4194304]{0:T(1024)(128)(4,1)S(1)}, s32[]{:S(2)}) async-start(s8[6291456]{0:T(1024)(128)(4,1)} %bitcast.5), calls=%async_computation | async-start | bytes 8388608
  206.6 29.5 %collective-permute-start.16 = (bf16[3,2,128,256]{3,2,1,0:T(8,128)(2,1)S(1)}, bf16[3,2,128,256]{3,2,1,0:T(8,128)(2,1)S(1)}, u32[]{:S(2)}, u32[]{:S(2)}) collective-permute-start(bf16[3,2,128,256]{3,2,1,0:T(8,128)(2,1)S(1)} %get-tuple-element.32), channel_id=1, source_target_pairs={{0,8},{4,12},{8,0},{12,4},{16,24},{20,28},{24,16},{28,20},{1,9},{5... | collective-permute-start | bytes 1179656 | tf_op jit(solution)/shard_map/ppermute | solution.py:66
  209.3 26.7 %collective-permute-start.18 = (bf16[3,2,128,256]{3,2,1,0:T(8,128)(2,1)S(1)}, bf16[3,2,128,256]{3,2,1,0:T(8,128)(2,1)S(1)}, u32[]{:S(2)}, u32[]{:S(2)}) collective-permute-start(bf16[3,2,128,256]{3,2,1,0:T(8,128)(2,1)S(1)} %get-tuple-element.34), channel_id=1, source_target_pairs={{0,12},{4,8},{8,4},{12,0},{16,28},{20,24},{24,20},{28,16},{1,13},{... | collective-permute-start | bytes 1179656 | tf_op jit(solution)/shard_map/ppermute | solution.py:66
  209.3 26.7 %collective-permute-start.15 = (bf16[3,2,128,256]{3,2,1,0:T(8,128)(2,1)S(1)}, bf16[3,2,128,256]{3,2,1,0:T(8,128)(2,1)S(1)}, u32[]{:S(2)}, u32[]{:S(2)}) collective-permute-start(bf16[3,2,128,256]{3,2,1,0:T(8,128)(2,1)S(1)} %get-tuple-element.31), channel_id=1, source_target_pairs={{0,4},{4,0},{8,12},{12,8},{16,20},{20,16},{24,28},{28,24},{1,5},{5... | collective-permute-start | bytes 1179656 | tf_op jit(solution)/shard_map/ppermute | solution.py:66
  212.0 24.0 %collective-permute-start.17 = (bf16[3,2,128,256]{3,2,1,0:T(8,128)(2,1)S(1)}, bf16[3,2,128,256]{3,2,1,0:T(8,128)(2,1)S(1)}, u32[]{:S(2)}, u32[]{:S(2)}) collective-permute-start(bf16[3,2,128,256]{3,2,1,0:T(8,128)(2,1)S(1)} %get-tuple-element.33), channel_id=1, source_target_pairs={{0,8},{4,12},{8,0},{12,4},{16,24},{20,28},{24,16},{28,20},{1,9},{5... | collective-permute-start | bytes 1179656 | tf_op jit(solution)/shard_map/ppermute | solution.py:66
  213.6 25.6 %collective-permute-start.19 = (bf16[3,2,128,256]{3,2,1,0:T(8,128)(2,1)S(1)}, bf16[3,2,128,256]{3,2,1,0:T(8,128)(2,1)S(1)}, u32[]{:S(2)}, u32[]{:S(2)}) collective-permute-start(bf16[3,2,128,256]{3,2,1,0:T(8,128)(2,1)S(1)} %get-tuple-element.35), channel_id=1, source_target_pairs={{0,12},{4,8},{8,4},{12,0},{16,28},{20,24},{24,20},{28,16},{1,13},{... | collective-permute-start | bytes 1179656 | tf_op jit(solution)/shard_map/ppermute | solution.py:66
  215.0 24.1 %slice-start.1 = ((s8[6291456]{0:T(1024)(128)(4,1)}), s8[2097152]{0:T(1024)(128)(4,1)S(1)}, s32[]{:S(2)}) async-start(s8[6291456]{0:T(1024)(128)(4,1)} %bitcast.5), calls=%async_computation.1 | async-start | bytes 4194304
  239.2 2.8 %copy-start.1 = (f32[3,2,256,1024]{3,2,1,0:T(8,128)S(1)}, f32[3,2,256,1024]{3,2,1,0:T(8,128)}, u32[]{:S(2)}) copy-start(f32[3,2,256,1024]{3,2,1,0:T(8,128)} %products.1.product) | copy-start | bytes 18874372

commit v2 on v1

--- a/solution.py
+++ b/solution.py
@@ -66,9 +66,33 @@
     return lax.ppermute(array, axis, [(i, i ^ bit) for i in range(size)])
 
 
-def section_kernel(group, split, where, state, slope, section, *chunks):
+def tie(arrays):
+    return lax.optimization_barrier(arrays)
+
+
+def row_bits(size):
+    return [1 << i for i in reversed(range(size.bit_length() - 1))]
+
+
+def tree(array, size, bits):
+    parts = {0: array}
+    for bit in bits:
+        for mask in list(parts):
+            parts[mask ^ bit] = swap(parts[mask], "row", size, bit)
+    return parts
+
+
+def section_kernel(group, split, where, state, slope, section, *outs):
     value = (state[...].astype(f32) + (0.5 * step_size) * slope[...]).astype(bf16)
     section[...] = value
+    a, ops = pl.program_id(0), len(outs) - group * split
+    singles, chunks = outs[:ops], outs[ops:]
+    for i, single in enumerate(singles):
+
+        @pl.when(a == i)
+        def _():
+            single[...] = value[0]
+
     width = chunks[0].shape[-1]
     height = chunks[0].shape[-2]
     for b in range(group):
@@ -83,23 +107,32 @@
     block = pl.BlockSpec((1, 1, rows, columns), lambda a, x, _: (a, x, 0, 0))
     chunk = pl.BlockSpec((1, 1, height, width), lambda a, x, _: (a, x, 0, 0))
     count = group * split
+
+    def single(i):
+        def place(a, x, _):
+            return jnp.where(a == i, x, jnp.where(a < i, 0, parts - 1)), 0, 0
+
+        return pl.BlockSpec((1, rows, columns), place)
+
     out = pl.pallas_call(
         functools.partial(section_kernel, group, split),
         grid_spec=pltpu.PrefetchScalarGridSpec(
             num_scalar_prefetch=1,
             grid=(ops, parts),
             in_specs=[block, block],
-            out_specs=[block] + [chunk] * count,
+            out_specs=[block] + [single(i) for i in range(ops)] + [chunk] * count,
         ),
         out_shape=[jax.ShapeDtypeStruct(state.shape, bf16)]
+        + [jax.ShapeDtypeStruct(state.shape[1:], bf16)] * ops
         + [jax.ShapeDtypeStruct((ops, parts, height, width), bf16)] * count,
-        compiler_params=params(24),
+        compiler_params=params(56),
         cost_estimate=pl.CostEstimate(
             flops=2 * state.size, bytes_accessed=10 * state.size, transcendentals=0
         ),
         name="section",
     )(place, state, prev_slope)
-    return out[0], [[out[1 + b * split + p] for b in range(group)] for p in range(split)]
+    singles, chunks = out[1 : 1 + ops], out[1 + ops :]
+    return out[0], singles, [[chunks[b * split + p] for b in range(group)] for p in range(split)]
 
 
 def fill_factors(vrows, vcols, coupling, factors):
@@ -246,101 +279,101 @@
     )(places, coupling, vrows, vcols, *chunks, received)
 
 
-def product_kernel(count, where, decay, h_own, s_own, *refs):
+def product_kernel(op, count, where, decay, h_own, s_own, *refs):
     s_parts, h_parts, out = refs[:count], refs[count : 2 * count], refs[2 * count]
     s_all, h_all = refs[2 * count + 1 :]
-    a = pl.program_id(1)
-    height = h_own.shape[1]
-
-    def place(b):
-        return pl.ds(pl.multiple_of((where[0] ^ b) * height, row_tile), height)
-
-    @pl.when(a == 0)
-    def _():
-        for b in range(count):
-            h_all[:, place(b), :] = h_parts[b][...]
-
+    height, depth = h_own.shape[1:]
     for b in range(count):
-        s_all[:, place(b), :] = s_parts[b][0]
-
-    def dot(left, right):
-        return jnp.dot(left, right, preferred_element_type=f32)
-
-    h_real, h_imag = h_own[0], h_own[1]
-    s_real, s_imag = s_own[a, 0], s_own[a, 1]
-    lost = decay[a]
-    imag = dot(h_real, s_all[1]) + dot(h_imag, s_all[0])
-    imag = imag - dot(s_real, h_all[1]) - dot(s_imag, h_all[0])
-    out[0, 0] = imag - lost * s_parts[0][0, 0].astype(f32)
-    real = dot(h_real, s_all[0]) - dot(h_imag, s_all[1])
-    real = real - dot(s_real, h_all[0]) + dot(s_imag, h_all[1])
-    out[0, 1] = -real - lost * s_parts[0][0, 1].astype(f32)
-
-
-def make_product(s_parts, h_parts, place, decay):
-    ops, _, rows, columns = s_parts[0].shape
-    count = len(s_parts)
+        rows = pl.ds(pl.multiple_of((where[0] ^ b) * height, row_tile), height)
+        h_all[:, rows, :] = h_parts[b][...]
+        s_all[:, rows, :] = s_parts[b][...].reshape(s_all.shape[0], height, -1)
+
+    def product(left, right):
+        left = left.reshape(2 * height, depth)
+        first = jnp.dot(left, right[0], preferred_element_type=f32)
+        second = jnp.dot(left, right[1], preferred_element_type=f32)
+        return first[:height] - second[height:], second[:height] + first[height:]
+
+    left_real, left_imag = product(h_own[...], s_all)
+    right_real, right_imag = product(s_own[0], h_all)
+    lost = decay[op]
+    own = s_parts[0]
+    out[0] = (left_imag - right_imag) - lost * own[0, 0].astype(f32)
+    out[1] = (right_real - left_real) - lost * own[0, 1].astype(f32)
+
+
+def make_product(op, near, far, h_parts, place, decay):
+    ops, _, rows, columns = near[0].shape
+    count = 2 * len(near)
     tile = min(columns, 256)
+    s_parts = [{**near, **far}[b] for b in range(count)]
+    held = pl.BlockSpec((2, rows, columns), lambda j: (0, 0, 0))
+    own = pl.BlockSpec((1, 2, rows, columns), lambda j: (op, 0, 0, 0))
+    three = pl.BlockSpec((2, rows, tile), lambda j: (0, 0, j))
+    four = pl.BlockSpec((1, 2, rows, tile), lambda j: (op, 0, 0, j))
     return pl.pallas_call(
-        functools.partial(product_kernel, count),
-        grid=(columns // tile, ops),
-        in_specs=[
-            scalars(),
-            scalars(),
-            pl.BlockSpec((2, rows, columns), lambda j, a: (0, 0, 0)),
-            pl.BlockSpec((ops, 2, rows, columns), lambda j, a: (0, 0, 0, 0)),
-        ]
-        + [pl.BlockSpec((1, 2, rows, tile), lambda j, a: (a, 0, 0, j))] * count
-        + [pl.BlockSpec((2, rows, tile), lambda j, a: (0, 0, j))] * count,
-        out_specs=pl.BlockSpec((1, 2, rows, tile), lambda j, a: (a, 0, 0, j)),
-        out_shape=jax.ShapeDtypeStruct((ops, 2, rows, columns), f32),
+        functools.partial(product_kernel, op, count),
+        grid=(columns // tile,),
+        in_specs=[scalars(), scalars(), held, own]
+        + [four if b in near else three for b in range(count)]
+        + [three] * count,
+        out_specs=three,
+        out_shape=jax.ShapeDtypeStruct((2, rows, columns), f32),
         scratch_shapes=[pltpu.VMEM((2, count * rows, tile), bf16)] * 2,
-        compiler_params=params(32),
+        compiler_params=params(48),
         cost_estimate=pl.CostEstimate(
-            flops=16 * ops * rows * columns * columns,
-            bytes_accessed=4 * count * (ops + 1) * rows * columns + 8 * ops * rows * columns,
+            flops=16 * rows * columns * columns,
+            bytes_accessed=8 * count * rows * columns + 16 * rows * columns,
             transcendentals=0,
         ),
         name="products",
-    )(place, decay, h_parts[0], s_parts[0], *s_parts, *h_parts)
-
-
-def final_kernel(group, split, where, product, accumulated, *refs):
-    sums, slope, total = refs[: group * split], refs[group * split], refs[group * split + 1]
-    b, a = pl.program_id(0), pl.program_id(1)
+    )(place, decay, h_parts[0], near[0], *s_parts, *h_parts)
+
+
+def final_kernel(ops, group, split, where, accumulated, *refs):
+    products, sums, (slope, total) = refs[:ops], refs[ops:-2], refs[-2:]
+    a, b = pl.program_id(0), pl.program_id(1)
     height = sums[0].shape[2]
-    for i in range(group):
-
-        @pl.when(b == i)
-        def _():
-            for p in range(split):
-                rows = slice(p * height, (p + 1) * height)
-                value = product[0, :, rows, :] + sums[i * split + p][a].astype(f32)
-                slope[0, :, rows, :] = value
-                total[0, :, rows, :] = accumulated[0, :, rows, :] + (step_size / 3.0) * value
-
-
-def make_final(product, accumulated, sums, place):
-    ops, parts, rows, columns = product.shape
+    for i in range(ops):
+        for k in range(group):
+
+            @pl.when(jnp.logical_and(a == i, b == k))
+            def _():
+                for p in range(split):
+                    rows = slice(p * height, (p + 1) * height)
+                    value = products[i][:, rows, :] + sums[k * split + p][i].astype(f32)
+                    slope[0, :, rows, :] = value
+                    total[0, :, rows, :] = accumulated[0, :, rows, :] + (step_size / 3.0) * value
+
+
+def make_final(products, accumulated, sums, place):
+    ops, parts, rows, columns = accumulated.shape
     split, group = len(sums), len(sums[0])
     width = columns // group
-    block = pl.BlockSpec((1, parts, rows, width), lambda b, a, g: (a, 0, 0, g[0] ^ b))
-    held = pl.BlockSpec(sums[0][0].shape, lambda b, a, g: (0, 0, 0, 0))
+    block = pl.BlockSpec((1, parts, rows, width), lambda a, b, g: (a, 0, 0, g[0] ^ b))
+    held = pl.BlockSpec(sums[0][0].shape, lambda a, b, g: (0, 0, 0, 0))
+
+    def single(i):
+        def place(a, b, g):
+            return 0, 0, g[0] ^ jnp.where(a == i, b, jnp.where(a < i, 0, group - 1))
+
+        return pl.BlockSpec((parts, rows, width), place)
+
     return pl.pallas_call(
-        functools.partial(final_kernel, group, split),
+        functools.partial(final_kernel, ops, group, split),
         grid_spec=pltpu.PrefetchScalarGridSpec(
             num_scalar_prefetch=1,
-            grid=(group, ops),
-            in_specs=[block, block] + [held] * (group * split),
+            grid=(ops, group),
+            in_specs=[block] + [single(i) for i in range(ops)] + [held] * (group * split),
             out_specs=[block, block],
         ),
-        out_shape=[jax.ShapeDtypeStruct(product.shape, f32)] * 2,
-        compiler_params=params(24),
+        out_shape=[jax.ShapeDtypeStruct(accumulated.shape, f32)] * 2,
+        compiler_params=params(56),
         cost_estimate=pl.CostEstimate(
-            flops=4 * product.size, bytes_accessed=18 * product.size, transcendentals=0
+            flops=4 * accumulated.size, bytes_accessed=18 * accumulated.size, transcendentals=0
         ),
         name="outputs",
-    )(place, product, accumulated, *[sums[p][b] for b in range(group) for p in range(split)])
+    )(place, accumulated, *products, *[sums[p][b] for b in range(group) for p in range(split)])
 
 
 def shards(
@@ -370,44 +403,77 @@
     own = hier_at % group
     own_place, row_place = own.reshape(1).astype(jnp.int32), row_at.reshape(1).astype(jnp.int32)
 
-    def gather_rows(array):
-        parts = {0: array}
-        bit = row // 2
-        while bit:
-            for mask in list(parts):
-                parts[mask ^ bit] = swap(parts[mask], "row", row, bit)
-            bit //= 2
-        return [parts[b] for b in range(row)]
-
-    h_parts = gather_rows(hamiltonian)
-    section, chunks = make_section(state, prev_slope, own_place, group, split)
-
-    everyone = lax.all_gather(occupation, "hier", axis=0, tiled=True)
+    half = {0: occupation}
+    for b in range(1, group):
+        half[b] = swap(occupation, "hier", hier, b)
+    bits = row_bits(row)
+    top, low = bits[0], bits[1:]
+    h_near, h_top = tree(hamiltonian, row, low), swap(hamiltonian, "row", row, top)
+    section, singles, chunks = make_section(state, prev_slope, own_place, group, split)
+    section, singles, chunks, half, h_near, h_top = tie(
+        (section, singles, chunks, half, h_near, h_top)
+    )
+
     known = jnp.asarray(np.array(table, np.int32))
-    same = jnp.all(everyone[:, None, :] == known[None, :, :], axis=2)
-    slot = jnp.sum(jnp.where(same, jnp.arange(hier * ops, dtype=jnp.int32)[:, None], 0), axis=0)
-    device = slot // ops
-    places = jnp.where(
-        device // group == hier_at // group,
-        ((device % group) ^ own) * ops + slot % ops,
-        group * ops,
-    ).astype(jnp.int32)
+    found = jnp.concatenate([half[b] for b in range(group)], axis=0)
+    same = jnp.all(found[None, :, :] == known[:, None, :], axis=2)
+    spot = jnp.arange(group * ops, dtype=jnp.int32)[None, :]
+    places = jnp.min(jnp.where(same, spot, group * ops), axis=1).astype(jnp.int32)
     vrows = lax.dynamic_slice_in_dim(couple_v, row_at * rows, rows, 1)[:, :, None]
     vcols = lax.dynamic_slice_in_dim(couple_v, own * width, width, 1)
     decay = jnp.sum(occupation.astype(f32) * damping[None, :], axis=1)
 
-    sums = []
-    for p in range(split):
-        here = vrows[:, p * height : (p + 1) * height]
-        got = [chunks[p][0]] + [swap(chunks[p][b], "hier", hier, b) for b in range(1, group)]
-        sent = make_partial(got, places, coupling, here, vcols, links, sides)
-        received = swap(sent, "hier", hier, group)
-        done = make_coupled(got, received, places, coupling, here, vcols, links, sides)
-        sums.append([done[0]] + [swap(done[b], "hier", hier, b) for b in range(1, group)])
-
-    s_parts = gather_rows(section)
-    product = make_product(s_parts, h_parts, row_place, decay)
-    slope, total = make_final(product, accumulated, sums, own_place)
+    heres = [vrows[:, p * height : (p + 1) * height] for p in range(split)]
+
+    def spread(p):
+        return [chunks[p][0]] + [swap(chunks[p][b], "hier", hier, b) for b in range(1, group)]
+
+    def partial(p):
+        return make_partial(got[p], places, coupling, heres[p], vcols, links, sides)
+
+    def coupled(p):
+        return make_coupled(got[p], received[p], places, coupling, heres[p], vcols, links, sides)
+
+    def gather_back(done):
+        return [done[0]] + [swap(done[b], "hier", hier, b) for b in range(1, group)]
+
+    def across(array):
+        return {mask ^ top: part for mask, part in tree(array, row, low).items()}
+
+    def product(a):
+        return make_product(a, near, far[a], h_parts, row_place, decay)
+
+    got, sent, received, sums, tops, far = [], [], [], [], [], []
+
+    got.append(spread(0))
+    tops.append(swap(singles[0], "row", row, top))
+    h_far = across(h_top)
+    got, tops, h_far, singles, chunks, section, places, heres, vcols, decay = tie(
+        (got, tops, h_far, singles, chunks, section, places, heres, vcols, decay)
+    )
+    h_parts = [{**h_near, **h_far}[b] for b in range(row)]
+
+    sent.append(partial(0))
+    received.append(swap(sent[0], "hier", hier, group))
+    got.append(spread(1))
+    tops.append(swap(singles[1], "row", row, top))
+    got, tops, received, singles, section = tie((got, tops, received, singles, section))
+
+    sent.append(partial(1))
+    received.append(swap(sent[1], "hier", hier, group))
+    tops.append(swap(singles[2], "row", row, top))
+    near = tree(section, row, low)
+    far = [across(tops[0]), across(tops[1])]
+    sums.append(coupled(0))
+    sums, near, far = tie((sums, near, far))
+    sums[0] = gather_back(sums[0])
+    products = [product(0), product(1)]
+    received, tops, sums, products = tie((received, tops, sums, products))
+
+    sums.append(gather_back(coupled(1)))
+    far.append(across(tops[2]))
+    products.append(product(2))
+    slope, total = make_final(products, accumulated, sums, own_place)
     return slope, total
 
 

time: 250 us -> 182 us (0.73)
  waiting for transfers between devices: 128 us -> 88.8 us
  blocking collectives: 38.4 us -> 0 us
  Pallas kernels: 44.1 us -> 59.1 us
  local copies, waits for them, and re-layouts: 13.8 us -> 3.72 us
  starting transfers between devices: 21.8 us -> 28.6 us
  other arithmetic: 2.79 us -> 0.25 us
    ppermute x20 -> x27, waiting for transfers between devices: 128 us -> 88.8 us  [swap(): return lax.ppermute(array, axis, [(i, i ^ bit) for i in range(size)])]
    all_gather x1 -> x0, blocking collectives: 38.4 us -> none  [shards(): everyone = lax.all_gather(occupation, 'hier', axis=0, tiled=True)]
    pallas_call x2 -> x4, Pallas kernels: 28.4 us -> 39.2 us  [the longest x3 25.4 us: make_product(): pl.pallas_call(functools.partial(product_kernel, op, count), grid=(column...]
    unnamed x18 -> x34, local copies, waits for them, and re-layouts: 11.2 us -> 3.34 us
    ppermute x20 -> x27, starting transfers between devices: 21.8 us -> 28.6 us  [swap(): return lax.ppermute(array, axis, [(i, i ^ bit) for i in range(size)])]
    pallas_call x1, Pallas kernels: 3.44 us -> 8.87 us  [make_section(): pl.pallas_call(functools.partial(section_kernel, group, split), grid_spec...]
  transfers between devices with their start and end apart: 20 -> 27, of which waited for: 8 -> 13; matrix products, arithmetic and copies ran while one was open for 4% -> 0% of each run, Pallas kernels for 13% -> 25%
where the time goes in v2:
time: 182 us; the launch traced here: 181 us
  waiting for transfers between devices  88.8 us (49%)
  Pallas kernels  59.1 us (32%)
  starting transfers between devices  28.6 us (16%)
  local copies, waits for them, and re-layouts  3.72 us (2%)
    ppermute x27, waiting for transfers between devices, swap(): return lax.ppermute(array, axis, [(i, i ^ bit) for i in range(size)])  88.8 us
    ppermute x27, starting transfers between devices, swap(): return lax.ppermute(array, axis, [(i, i ^ bit) for i in range(size)])  28.6 us
    pallas_call x3, Pallas kernels, make_product(): pl.pallas_call(functools.partial(product_kernel, op, count), grid=(column...  25.4 us
    pallas_call x1, Pallas kernels, make_final(): pl.pallas_call(functools.partial(final_kernel, ops, group, split), grid_s...  13.8 us
    pallas_call x1, Pallas kernels, make_section(): pl.pallas_call(functools.partial(section_kernel, group, split), grid_spec...  8.87 us
    pallas_call x2, Pallas kernels, make_coupled(): pl.pallas_call(functools.partial(coupled_kernel, links, sides, group), in...  6.91 us
    pallas_call x2, Pallas kernels, make_partial(): pl.pallas_call(functools.partial(partial_kernel, links, sides, group), in...  4.14 us
  transfers between devices with their start and end apart: 27, of which 13 were waited for; matrix products, arithmetic and copies ran while one was open for 0% of the time, Pallas kernels for 25%

profile of v2, /device:TPU:0, one launch (start us, length us, event | category | flops | bytes accessed | tf_op | source)
XLA Modules:
  0.0 181.4 jit_solution(517611809630352757)
XLA Ops:
  0.6 0.5 collective-permute-start.3
  1.1 2.6 %collective-permute-start.4 = (bf16[2,256,1024]{2,1,0:T(8,128)(2,1)}, bf16[2,256,1024]{2,1,0:T(8,128)(2,1)S(1)}, u32[]{:S(2)}, u32[]{:S(2)}) collective-permute-start(bf16[2,256,1024]{2,1,0:T(8,128)(2,1)} %refs_4_.2), channel_id=1, source_target_pairs={{0,2},{1,3},{2,0},{3,1},{4,6},{5,7},{6,4},{7,5},{8,10},{9,11},{10,... | collective-permute-start | bytes 3145736 | tf_op jit(solution)/shard_map/ppermute | solution.py:66
  3.7 2.5 %collective-permute-start.2 = (s32[3,6]{1,0:T(4,128)}, s32[3,6]{1,0:T(4,128)S(1)}, u32[]{:S(2)}, u32[]{:S(2)}) collective-permute-start(s32[3,6]{1,0:T(4,128)} %param.18), channel_id=1, source_target_pairs={{0,12},{4,8},{8,4},{12,0},{16,28},{20,24},{24,20},{28,16},{1,13},{... | collective-permute-start | bytes 224 | tf_op jit(solution)/shard_map/ppermute | solution.py:66
  6.2 0.4 collective-permute-start.1
  6.7 0.5 collective-permute-start
  7.3 8.9 %section.1 = (bf16[3,2,256,1024]{3,2,1,0:T(8,128)(2,1)}, bf16[2,256,1024]{2,1,0:T(8,128)(2,1)}, bf16[2,256,1024]{2,1,0:T(8,128)(2,1)}, bf16[2,256,1024]{2,1,0:T(...) custom-call(s32[1]{0:T(128)} %bitcast.where, ...), custom_call_target="tpu_custom_call" | custom-call | flops 3145728 | bytes 15728640 | tf_op jit(solution)/shard_map/section/pallas_call | solution.py:117
  16.1 0.0 collective-permute-done.2
  16.2 0.0 collective-permute-done.1
  16.2 0.0 collective-permute-done.3.refs_5_
  16.2 11.5 %collective-permute-done.4.refs_6_ = bf16[2,256,1024]{2,1,0:T(8,128)(2,1)S(1)} collective-permute-done((bf16[2,256,1024]{2,1,0:T(8,128)(2,1)}, bf16[2,256,1024]{2,1,0:T(8,128)(2,1)S(1)}, u32[]{:S(2)}, u32[]{:S(2)}) %collective-permute-start.4) | collective-permute-done | bytes 1048608 | tf_op jit(solution)/shard_map/ppermute | solution.py:66
  27.7 1.8 collective-permute-start.8
  29.5 0.0 collective-permute-start.9
  29.5 1.6 collective-permute-start.5
  31.0 1.6 collective-permute-start.6
  32.6 0.4 collective-permute-start.7
  33.0 0.1 multiply_reduce_fusion.decay
  33.2 0.2 copy.16.vrows
  33.4 0.2 copy.15.vrows
  33.6 0.1 compare_reduce_fusion
  33.7 7.6 %collective-permute-done.5.refs_1_ = bf16[3,2,128,256]{3,2,1,0:T(8,128)(2,1)} collective-permute-done((bf16[3,2,128,256]{3,2,1,0:T(8,128)(2,1)}, bf16[3,2,128,256]{3,2,1,0:T(8,128)(2,1)}, u32[]{:S(2)}, u32[]{:S(2)}) %collective-permute-start.5) | collective-permute-done | bytes 393248 | tf_op jit(solution)/shard_map/ppermute | solution.py:66
  41.3 2.0 %collective-permute-done.6.refs_2_ = bf16[3,2,128,256]{3,2,1,0:T(8,128)(2,1)} collective-permute-done((bf16[3,2,128,256]{3,2,1,0:T(8,128)(2,1)}, bf16[3,2,128,256]{3,2,1,0:T(8,128)(2,1)}, u32[]{:S(2)}, u32[]{:S(2)}) %collective-permute-start.6) | collective-permute-done | bytes 393248 | tf_op jit(solution)/shard_map/ppermute | solution.py:66
  43.3 7.6 %collective-permute-done.7.refs_3_ = bf16[3,2,128,256]{3,2,1,0:T(8,128)(2,1)} collective-permute-done((bf16[3,2,128,256]{3,2,1,0:T(8,128)(2,1)}, bf16[3,2,128,256]{3,2,1,0:T(8,128)(2,1)}, u32[]{:S(2)}, u32[]{:S(2)}) %collective-permute-start.7) | collective-permute-done | bytes 393248 | tf_op jit(solution)/shard_map/ppermute | solution.py:66
  50.9 2.0 %collective-permute-done.8.refs_2_ = bf16[2,256,1024]{2,1,0:T(8,128)(2,1)} collective-permute-done((bf16[2,256,1024]{2,1,0:T(8,128)(2,1)}, bf16[2,256,1024]{2,1,0:T(8,128)(2,1)}, u32[]{:S(2)}, u32[]{:S(2)}) %collective-permute-start.8) | collective-permute-done | bytes 1048608 | tf_op jit(solution)/shard_map/ppermute | solution.py:66
  52.9 1.6 collective-permute-start.13
  54.5 1.0 copy-done.2
  55.5 2.4 %partial_sums.2 = bf16[6,2,128,256]{3,2,1,0:T(8,128)(2,1)S(1)} custom-call(s32[24]{0:T(128)S(1)} %select_reduce_fusion.places, f32[2,6]{1,0:T(2,128)S(1)} %copy-done.5, f32[6,128,1]{2,1,0:T(8,128)S(1)} %copy.15.vrows, f32[6,256]{1,0:T(8,128)S(1)} %get-tuple-element.132.vcols, bf16[3,2,128,256]{3,2,1,0:T(8,128)(2,1)S(1)} %copy-done.2, ...), custom_call_target="tpu_custom_call" | custom-call | flops 7864320 | bytes 2359296 | tf_op jit(solution)/shard_map/partial_sums/pallas_call | solution.py:242
  57.9 0.0 copy-start
  57.9 2.6 %collective-permute-start.14 = (bf16[6,2,128,256]{3,2,1,0:T(8,128)(2,1)S(1)}, bf16[6,2,128,256]{3,2,1,0:T(8,128)(2,1)S(1)}, u32[]{:S(2)}, u32[]{:S(2)}) collective-permute-start(bf16[6,2,128,256]{3,2,1,0:T(8,128)(2,1)S(1)} %partial_sums.2), channel_id=1, source_target_pairs={{0,16},{4,20},{8,24},{12,28},{16,0},{20,4},{24,8},{28,12},{1,17},{... | collective-permute-start | bytes 2359304 | tf_op jit(solution)/shard_map/ppermute | solution.py:66
  60.6 1.5 collective-permute-start.10
  62.0 1.6 collective-permute-start.11
  63.6 0.4 collective-permute-start.12
  64.0 7.9 %collective-permute-done.10.refs_1_ = bf16[3,2,128,256]{3,2,1,0:T(8,128)(2,1)S(1)} collective-permute-done((bf16[3,2,128,256]{3,2,1,0:T(8,128)(2,1)}, bf16[3,2,128,256]{3,2,1,0:T(8,128)(2,1)S(1)}, u32[]{:S(2)}, u32[]{:S(2)}) %collective-permute-start.10) | collective-permute-done | bytes 393248 | tf_op jit(solution)/shard_map/ppermute | solution.py:66
  71.9 15.2 %collective-permute-done.11.refs_2_ = bf16[3,2,128,256]{3,2,1,0:T(8,128)(2,1)S(1)} collective-permute-done((bf16[3,2,128,256]{3,2,1,0:T(8,128)(2,1)}, bf16[3,2,128,256]{3,2,1,0:T(8,128)(2,1)S(1)}, u32[]{:S(2)}, u32[]{:S(2)}) %collective-permute-start.11) | collective-permute-done | bytes 393248 | tf_op jit(solution)/shard_map/ppermute | solution.py:66
  87.1 8.3 %collective-permute-done.12.refs_3_ = bf16[3,2,128,256]{3,2,1,0:T(8,128)(2,1)S(1)} collective-permute-done((bf16[3,2,128,256]{3,2,1,0:T(8,128)(2,1)}, bf16[3,2,128,256]{3,2,1,0:T(8,128)(2,1)S(1)}, u32[]{:S(2)}, u32[]{:S(2)}) %collective-permute-start.12) | collective-permute-done | bytes 393248 | tf_op jit(solution)/shard_map/ppermute | solution.py:66
  95.3 0.0 collective-permute-start.17
  95.4 0.5 collective-permute-start.18
  95.9 0.1 collective-permute-start.19
  95.9 0.5 collective-permute-start.16
  96.4 1.7 partial_sums.3
  98.2 0.9 collective-permute-start.15
  99.1 3.8 %coupling_sums.2 = (bf16[3,2,128,256]{3,2,1,0:T(8,128)(2,1)S(1)}, bf16[3,2,128,256]{3,2,1,0:T(8,128)(2,1)S(1)}, bf16[3,2,128,256]{3,2,1,0:T(8,128)(2,1)S(1)}, bf16[3,2,128,256]{3,2,1,0:T(8,128)(2,1)S(1)}) custom-call(s32[24]{0:T(128)S(1)} %select_reduce_fusion.places, f32[2,6]{1,0:T(2,128)S(1)} %copy-done.5, f32[6,128,1]{2,1,0:T(8,128)S(1)} %copy.15.vrows, ...), custom_call_target="tpu_custom_call" | custom-call | flops 15728640 | bytes 3932160 | tf_op jit(solution)/shard_map/coupling_sums/pallas_call | solution.py:263
  102.9 0.8 copy-done.3
  103.7 0.5 collective-permute-done.18.refs_3_
  104.2 1.6 collective-permute-start.20
  105.8 1.6 collective-permute-start.21
  107.4 0.4 collective-permute-start.22
  107.8 8.5 %products.3.refs_0_ = f32[2,256,1024]{2,1,0:T(8,128)} custom-call(s32[1]{0:T(128)} %bitcast.2.where, f32[3]{0:T(128)S(1)} %multiply_reduce_fusion.decay, bf16[2,256,1024]{2,1,0:T(8,128)(2,1)S(1)} %copy-done, bf16[3,2,256,1024]{3,2,1,0:T(8,128)(2,1)} %get-tuple-element.159.s_own.refs_0_, bf16[3,2,256,1024]{3,2,1,0:T(8,128)(2,1)} %get-tuple-element.159.s_own.refs_0_, ...), custom_call_target="tpu_custom_call" | custom-call | flops 4294967296 | bytes 12582912 | tf_op jit(solution)/shard_map/products/pallas_call | solution.py:314
  116.3 8.5 %products.4.refs_1_ = f32[2,256,1024]{2,1,0:T(8,128)} custom-call(s32[1]{0:T(128)} %bitcast.2.where, f32[3]{0:T(128)S(1)} %multiply_reduce_fusion.decay, bf16[2,256,1024]{2,1,0:T(8,128)(2,1)S(1)} %copy-done, bf16[3,2,256,1024]{3,2,1,0:T(8,128)(2,1)} %get-tuple-element.159.s_own.refs_0_, bf16[3,2,256,1024]{3,2,1,0:T(8,128)(2,1)} %get-tuple-element.159.s_own.refs_0_, ...), custom_call_target="tpu_custom_call" | custom-call | flops 4294967296 | bytes 12582912 | tf_op jit(solution)/shard_map/products/pallas_call | solution.py:314
  124.8 10.9 %collective-permute-done.15.refs_4_ = bf16[6,2,128,256]{3,2,1,0:T(8,128)(2,1)S(1)} collective-permute-done((bf16[6,2,128,256]{3,2,1,0:T(8,128)(2,1)S(1)}, bf16[6,2,128,256]{3,2,1,0:T(8,128)(2,1)S(1)}, u32[]{:S(2)}, u32[]{:S(2)}) %collective-permute-start.15) | collective-permute-done | bytes 786464 | tf_op jit(solution)/shard_map/ppermute | solution.py:66
  135.7 0.0 collective-permute-done.20.refs_5_
  135.7 0.0 collective-permute-done.21.refs_7_
  135.7 6.1 %collective-permute-done.22.refs_9_ = bf16[3,2,128,256]{3,2,1,0:T(8,128)(2,1)S(1)} collective-permute-done((bf16[3,2,128,256]{3,2,1,0:T(8,128)(2,1)S(1)}, bf16[3,2,128,256]{3,2,1,0:T(8,128)(2,1)S(1)}, u32[]{:S(2)}, u32[]{:S(2)}) %collective-permute-start.22) | collective-permute-done | bytes 393248 | tf_op jit(solution)/shard_map/ppermute | solution.py:66
  141.8 0.0 collective-permute-start.23
  141.8 3.1 %coupling_sums.3 = (bf16[3,2,128,256]{3,2,1,0:T(8,128)(2,1)S(1)}, bf16[3,2,128,256]{3,2,1,0:T(8,128)(2,1)S(1)}, bf16[3,2,128,256]{3,2,1,0:T(8,128)(2,1)S(1)}, bf16[3,2,128,256]{3,2,1,0:T(8,128)(2,1)S(1)}) custom-call(s32[24]{0:T(128)S(1)} %select_reduce_fusion.places, f32[2,6]{1,0:T(2,128)S(1)} %copy-done.5, f32[6,128,1]{2,1,0:T(8,128)S(1)} %copy.16.vrows, ...), custom_call_target="tpu_custom_call" | custom-call | flops 15728640 | bytes 3932160 | tf_op jit(solution)/shard_map/coupling_sums/pallas_call | solution.py:263
  144.9 0.8 copy-done.4
  145.7 1.1 collective-permute-start.24
  146.8 2.4 %collective-permute-start.26 = (bf16[3,2,128,256]{3,2,1,0:T(8,128)(2,1)S(1)}, bf16[3,2,128,256]{3,2,1,0:T(8,128)(2,1)S(1)}, u32[]{:S(2)}, u32[]{:S(2)}) collective-permute-start(bf16[3,2,128,256]{3,2,1,0:T(8,128)(2,1)S(1)} %get-tuple-element.179), channel_id=1, source_target_pairs={{0,12},{4,8},{8,4},{12,0},{16,28},{20,24},{24,20},{28,16},{1,13},{... | collective-permute-start | bytes 1179656 | tf_op jit(solution)/shard_map/ppermute | solution.py:66
  149.2 0.0 collective-permute-done.23.refs_3_
  149.2 8.5 %products.5.refs_2_ = f32[2,256,1024]{2,1,0:T(8,128)} custom-call(s32[1]{0:T(128)} %bitcast.2.where, f32[3]{0:T(128)S(1)} %multiply_reduce_fusion.decay, bf16[2,256,1024]{2,1,0:T(8,128)(2,1)S(1)} %copy-done, bf16[3,2,256,1024]{3,2,1,0:T(8,128)(2,1)} %get-tuple-element.159.s_own.refs_0_, bf16[3,2,256,1024]{3,2,1,0:T(8,128)(2,1)} %get-tuple-element.159.s_own.refs_0_, ...), custom_call_target="tpu_custom_call" | custom-call | flops 4294967296 | bytes 12582912 | tf_op jit(solution)/shard_map/products/pallas_call | solution.py:314
  157.7 0.0 collective-permute-done.24.refs_6_
  157.7 1.0 collective-permute-done.25.refs_8_
  158.8 8.1 %collective-permute-done.26.refs_10_ = bf16[3,2,128,256]{3,2,1,0:T(8,128)(2,1)S(1)} collective-permute-done((bf16[3,2,128,256]{3,2,1,0:T(8,128)(2,1)S(1)}, bf16[3,2,128,256]{3,2,1,0:T(8,128)(2,1)S(1)}, u32[]{:S(2)}, u32[]{:S(2)}) %collective-permute-start.26) | collective-permute-done | bytes 393248 | tf_op jit(solution)/shard_map/ppermute | solution.py:66
  166.9 0.7 copy-done.12
  167.6 13.8 %outputs.1 = (f32[3,2,256,1024]{3,2,1,0:T(8,128)}, f32[3,2,256,1024]{3,2,1,0:T(8,128)}) custom-call(s32[1]{0:T(128)} %bitcast.where, f32[3,2,256,1024]{3,2,1,0:T(8,128)} %accumulated.1, f32[2,256,1024]{2,1,0:T(8,128)} %products.3.refs_0_, f32[2,256,1024]{2,1,0:T(8,128)} %products.4.refs_1_, f32[2,256,1024]{2,1,0:T(8,128)} %products.5.refs_2_, ...), custom_call_target="tpu_custom_call" | custom-call | flops 6291456 | bytes 28311552 | tf_op jit(solution)/shard_map/outputs/pallas_call | solution.py:362
  (41 shorter events, 0.1 us)
Async XLA Ops:
  0.6 15.5 %collective-permute-start.3 = (bf16[2,256,1024]{2,1,0:T(8,128)(2,1)}, bf16[2,256,1024]{2,1,0:T(8,128)(2,1)S(1)}, u32[]{:S(2)}, u32[]{:S(2)}) collective-permute-start(bf16[2,256,1024]{2,1,0:T(8,128)(2,1)} %refs_4_.2), channel_id=1, source_target_pairs={{0,1},{1,0},{2,3},{3,2},{4,5},{5,4},{6,7},{7,6},{8,9},{9,8},{10,11... | collective-permute-start | bytes 3145736 | tf_op jit(solution)/shard_map/ppermute | solution.py:66
  1.1 26.6 %collective-permute-start.4 = (bf16[2,256,1024]{2,1,0:T(8,128)(2,1)}, bf16[2,256,1024]{2,1,0:T(8,128)(2,1)S(1)}, u32[]{:S(2)}, u32[]{:S(2)}) collective-permute-start(bf16[2,256,1024]{2,1,0:T(8,128)(2,1)} %refs_4_.2), channel_id=1, source_target_pairs={{0,2},{1,3},{2,0},{3,1},{4,6},{5,7},{6,4},{7,5},{8,10},{9,11},{10,... | collective-permute-start | bytes 3145736 | tf_op jit(solution)/shard_map/ppermute | solution.py:66
  3.7 12.4 %collective-permute-start.2 = (s32[3,6]{1,0:T(4,128)}, s32[3,6]{1,0:T(4,128)S(1)}, u32[]{:S(2)}, u32[]{:S(2)}) collective-permute-start(s32[3,6]{1,0:T(4,128)} %param.18), channel_id=1, source_target_pairs={{0,12},{4,8},{8,4},{12,0},{16,28},{20,24},{24,20},{28,16},{1,13},{... | collective-permute-start | bytes 224 | tf_op jit(solution)/shard_map/ppermute | solution.py:66
  6.2 9.9 %collective-permute-start.1 = (s32[3,6]{1,0:T(4,128)}, s32[3,6]{1,0:T(4,128)S(1)}, u32[]{:S(2)}, u32[]{:S(2)}) collective-permute-start(s32[3,6]{1,0:T(4,128)} %param.18), channel_id=1, source_target_pairs={{0,8},{4,12},{8,0},{12,4},{16,24},{20,28},{24,16},{28,20},{1,9},{5... | collective-permute-start | bytes 224 | tf_op jit(solution)/shard_map/ppermute | solution.py:66
  6.7 9.5 %collective-permute-start = (s32[3,6]{1,0:T(4,128)}, s32[3,6]{1,0:T(4,128)S(1)}, u32[]{:S(2)}, u32[]{:S(2)}) collective-permute-start(s32[3,6]{1,0:T(4,128)} %param.18), channel_id=1, source_target_pairs={{0,4},{4,0},{8,12},{12,8},{16,20},{20,16},{24,28},{28,24},{1,5},{5... | collective-permute-start | bytes 224 | tf_op jit(solution)/shard_map/ppermute | solution.py:66
  7.2 22.2 %copy-start.13 = (f32[6,1024]{1,0:T(8,128)S(1)}, f32[6,1024]{1,0:T(8,128)}, u32[]{:S(2)}) copy-start(f32[6,1024]{1,0:T(8,128)} %param.15) | copy-start | bytes 73732
  7.2 25.8 %copy-start.14 = (s32[3,6]{1,0:T(4,128)S(1)}, s32[3,6]{1,0:T(4,128)}, u32[]{:S(2)}) copy-start(s32[3,6]{1,0:T(4,128)} %param.18) | copy-start | bytes 220
  7.2 25.8 %copy-start.16 = (f32[6]{0:T(128)S(1)}, f32[6]{0:T(128)}, u32[]{:S(2)}) copy-start(f32[6]{0:T(128)} %param.17) | copy-start | bytes 76
  7.2 26.3 %copy-start.15 = (s32[24,6]{0,1:T(8,128)S(1)}, s32[24,6]{0,1:T(8,128)}, u32[]{:S(2)}) copy-start(s32[24,6]{0,1:T(8,128)} %constant.37.clone) | copy-start | bytes 1732
  7.2 47.3 %copy-start.5 = (f32[2,6]{1,0:T(2,128)S(1)}, f32[2,6]{1,0:T(2,128)}, u32[]{:S(2)}) copy-start(f32[2,6]{1,0:T(2,128)} %coupling.7) | copy-start | bytes 148
  16.1 80.3 %copy-start.1 = (bf16[3,2,128,256]{3,2,1,0:T(8,128)(2,1)S(1)}, bf16[3,2,128,256]{3,2,1,0:T(8,128)(2,1)}, u32[]{:S(2)}) copy-start(bf16[3,2,128,256]{3,2,1,0:T(8,128)(2,1)} %get-tuple-element.137.refs_0_) | copy-start | bytes 1179652
  27.7 25.2 %collective-permute-start.8 = (bf16[2,256,1024]{2,1,0:T(8,128)(2,1)}, bf16[2,256,1024]{2,1,0:T(8,128)(2,1)}, u32[]{:S(2)}, u32[]{:S(2)}) collective-permute-start(bf16[2,256,1024]{2,1,0:T(8,128)(2,1)} %get-tuple-element.107), channel_id=1, source_target_pairs={{0,2},{1,3},{2,0},{3,1},{4,6},{5,7},{6,4},{7,5},{8,10},{9,11},{10,... | collective-permute-start | bytes 3145736 | tf_op jit(solution)/shard_map/ppermute | solution.py:66
  29.5 23.5 %collective-permute-start.9 = (bf16[2,256,1024]{2,1,0:T(8,128)(2,1)S(1)}, bf16[2,256,1024]{2,1,0:T(8,128)(2,1)}, u32[]{:S(2)}, u32[]{:S(2)}) collective-permute-start(bf16[2,256,1024]{2,1,0:T(8,128)(2,1)S(1)} %collective-permute-done.4.refs_6_), channel_id=1, source_target_pairs={{0,1},{1,0},{2,3},{3,2},{4,5},{5,4},{6,7},{7,6},{8,9},{9,8},{10,11... | collective-permute-start | bytes 3145736 | tf_op jit(solution)/shard_map/ppermute | solution.py:66
  29.5 11.8 %collective-permute-start.5 = (bf16[3,2,128,256]{3,2,1,0:T(8,128)(2,1)}, bf16[3,2,128,256]{3,2,1,0:T(8,128)(2,1)}, u32[]{:S(2)}, u32[]{:S(2)}) collective-permute-start(bf16[3,2,128,256]{3,2,1,0:T(8,128)(2,1)} %get-tuple-element.104), channel_id=1, source_target_pairs={{0,4},{4,0},{8,12},{12,8},{16,20},{20,16},{24,28},{28,24},{1,5},{5... | collective-permute-start | bytes 1179656 | tf_op jit(solution)/shard_map/ppermute | solution.py:66
  31.0 12.3 %collective-permute-start.6 = (bf16[3,2,128,256]{3,2,1,0:T(8,128)(2,1)}, bf16[3,2,128,256]{3,2,1,0:T(8,128)(2,1)}, u32[]{:S(2)}, u32[]{:S(2)}) collective-permute-start(bf16[3,2,128,256]{3,2,1,0:T(8,128)(2,1)} %get-tuple-element.105), channel_id=1, source_target_pairs={{0,8},{4,12},{8,0},{12,4},{16,24},{20,28},{24,16},{28,20},{1,9},{5... | collective-permute-start | bytes 1179656 | tf_op jit(solution)/shard_map/ppermute | solution.py:66
  32.6 18.3 %collective-permute-start.7 = (bf16[3,2,128,256]{3,2,1,0:T(8,128)(2,1)}, bf16[3,2,128,256]{3,2,1,0:T(8,128)(2,1)}, u32[]{:S(2)}, u32[]{:S(2)}) collective-permute-start(bf16[3,2,128,256]{3,2,1,0:T(8,128)(2,1)} %get-tuple-element.106), channel_id=1, source_target_pairs={{0,12},{4,8},{8,4},{12,0},{16,28},{20,24},{24,20},{28,16},{1,13},{... | collective-permute-start | bytes 1179656 | tf_op jit(solution)/shard_map/ppermute | solution.py:66
  52.9 42.4 %collective-permute-start.13 = (bf16[2,256,1024]{2,1,0:T(8,128)(2,1)}, bf16[2,256,1024]{2,1,0:T(8,128)(2,1)S(1)}, u32[]{:S(2)}, u32[]{:S(2)}) collective-permute-start(bf16[2,256,1024]{2,1,0:T(8,128)(2,1)} %get-tuple-element.129), channel_id=1, source_target_pairs={{0,2},{1,3},{2,0},{3,1},{4,6},{5,7},{6,4},{7,5},{8,10},{9,11},{10,... | collective-permute-start | bytes 3145736 | tf_op jit(solution)/shard_map/ppermute | solution.py:66
  54.5 1.0 copy-start.2
  57.9 49.9 %copy-start = (bf16[2,256,1024]{2,1,0:T(8,128)(2,1)S(1)}, bf16[2,256,1024]{2,1,0:T(8,128)(2,1)}, u32[]{:S(2)}) copy-start(bf16[2,256,1024]{2,1,0:T(8,128)(2,1)} %refs_4_.2) | copy-start | bytes 3145732
  57.9 37.4 %collective-permute-start.14 = (bf16[6,2,128,256]{3,2,1,0:T(8,128)(2,1)S(1)}, bf16[6,2,128,256]{3,2,1,0:T(8,128)(2,1)S(1)}, u32[]{:S(2)}, u32[]{:S(2)}) collective-permute-start(bf16[6,2,128,256]{3,2,1,0:T(8,128)(2,1)S(1)} %partial_sums.2), channel_id=1, source_target_pairs={{0,16},{4,20},{8,24},{12,28},{16,0},{20,4},{24,8},{28,12},{1,17},{... | collective-permute-start | bytes 2359304 | tf_op jit(solution)/shard_map/ppermute | solution.py:66
  60.6 11.4 %collective-permute-start.10 = (bf16[3,2,128,256]{3,2,1,0:T(8,128)(2,1)}, bf16[3,2,128,256]{3,2,1,0:T(8,128)(2,1)S(1)}, u32[]{:S(2)}, u32[]{:S(2)}) collective-permute-start(bf16[3,2,128,256]{3,2,1,0:T(8,128)(2,1)} %get-tuple-element.125), channel_id=1, source_target_pairs={{0,4},{4,0},{8,12},{12,8},{16,20},{20,16},{24,28},{28,24},{1,5},{5... | collective-permute-start | bytes 1179656 | tf_op jit(solution)/shard_map/ppermute | solution.py:66
  62.0 25.0 %collective-permute-start.11 = (bf16[3,2,128,256]{3,2,1,0:T(8,128)(2,1)}, bf16[3,2,128,256]{3,2,1,0:T(8,128)(2,1)S(1)}, u32[]{:S(2)}, u32[]{:S(2)}) collective-permute-start(bf16[3,2,128,256]{3,2,1,0:T(8,128)(2,1)} %get-tuple-element.126), channel_id=1, source_target_pairs={{0,8},{4,12},{8,0},{12,4},{16,24},{20,28},{24,16},{28,20},{1,9},{5... | collective-permute-start | bytes 1179656 | tf_op jit(solution)/shard_map/ppermute | solution.py:66
  63.6 31.7 %collective-permute-start.12 = (bf16[3,2,128,256]{3,2,1,0:T(8,128)(2,1)}, bf16[3,2,128,256]{3,2,1,0:T(8,128)(2,1)S(1)}, u32[]{:S(2)}, u32[]{:S(2)}) collective-permute-start(bf16[3,2,128,256]{3,2,1,0:T(8,128)(2,1)} %get-tuple-element.127), channel_id=1, source_target_pairs={{0,12},{4,8},{8,4},{12,0},{16,28},{20,24},{24,20},{28,16},{1,13},{... | collective-permute-start | bytes 1179656 | tf_op jit(solution)/shard_map/ppermute | solution.py:66
  95.3 8.9 %collective-permute-start.17 = (bf16[3,2,256,1024]{3,2,1,0:T(8,128)(2,1)}, bf16[3,2,256,1024]{3,2,1,0:T(8,128)(2,1)S(1)}, u32[]{:S(2)}, u32[]{:S(2)}) collective-permute-start(bf16[3,2,256,1024]{3,2,1,0:T(8,128)(2,1)} %get-tuple-element.159.s_own.refs_0_), channel_id=1, source_target_pairs={{0,1},{1,0},{2,3},{3,2},{4,5},{5,4},{6,7},{7,6},{8,9},{9,8},{10,11... | collective-permute-start | bytes 9437192 | tf_op jit(solution)/shard_map/ppermute | solution.py:66
  95.4 8.9 %collective-permute-start.18 = (bf16[2,256,1024]{2,1,0:T(8,128)(2,1)}, bf16[2,256,1024]{2,1,0:T(8,128)(2,1)S(1)}, u32[]{:S(2)}, u32[]{:S(2)}) collective-permute-start(bf16[2,256,1024]{2,1,0:T(8,128)(2,1)} %collective-permute-done.8.refs_2_), channel_id=1, source_target_pairs={{0,1},{1,0},{2,3},{3,2},{4,5},{5,4},{6,7},{7,6},{8,9},{9,8},{10,11... | collective-permute-start | bytes 3145736 | tf_op jit(solution)/shard_map/ppermute | solution.py:66
  95.9 8.4 %collective-permute-start.19 = (bf16[2,256,1024]{2,1,0:T(8,128)(2,1)S(1)}, bf16[2,256,1024]{2,1,0:T(8,128)(2,1)S(1)}, u32[]{:S(2)}, u32[]{:S(2)}) collective-permute-start(bf16[2,256,1024]{2,1,0:T(8,128)(2,1)S(1)} %collective-permute-done.13.refs_2_), channel_id=1, source_target_pairs={{0,1},{1,0},{2,3},{3,2},{4,5},{5,4},{6,7},{7,6},{8,9},{9,8},{10,11... | collective-permute-start | bytes 3145736 | tf_op jit(solution)/shard_map/ppermute | solution.py:66
  95.9 39.8 %collective-permute-start.16 = (bf16[2,256,1024]{2,1,0:T(8,128)(2,1)}, bf16[2,256,1024]{2,1,0:T(8,128)(2,1)S(1)}, u32[]{:S(2)}, u32[]{:S(2)}) collective-permute-start(bf16[2,256,1024]{2,1,0:T(8,128)(2,1)} %get-tuple-element.143), channel_id=1, source_target_pairs={{0,2},{1,3},{2,0},{3,1},{4,6},{5,7},{6,4},{7,5},{8,10},{9,11},{10,... | collective-permute-start | bytes 3145736 | tf_op jit(solution)/shard_map/ppermute | solution.py:66
  98.2 37.5 %collective-permute-start.15 = (bf16[6,2,128,256]{3,2,1,0:T(8,128)(2,1)S(1)}, bf16[6,2,128,256]{3,2,1,0:T(8,128)(2,1)S(1)}, u32[]{:S(2)}, u32[]{:S(2)}) collective-permute-start(bf16[6,2,128,256]{3,2,1,0:T(8,128)(2,1)S(1)} %partial_sums.3), channel_id=1, source_target_pairs={{0,16},{4,20},{8,24},{12,28},{16,0},{20,4},{24,8},{28,12},{1,17},{... | collective-permute-start | bytes 2359304 | tf_op jit(solution)/shard_map/ppermute | solution.py:66
  102.9 0.8 copy-start.3
  104.2 3.6 %copy-start.6 = (bf16[3,2,256,1024]{3,2,1,0:T(8,128)(2,1)}, bf16[3,2,256,1024]{3,2,1,0:T(8,128)(2,1)S(1)}, u32[]{:S(2)}) copy-start(bf16[3,2,256,1024]{3,2,1,0:T(8,128)(2,1)S(1)} %collective-permute-done.17.refs_1_) | copy-start | bytes 9437188
  104.2 31.5 %collective-permute-start.20 = (bf16[3,2,128,256]{3,2,1,0:T(8,128)(2,1)S(1)}, bf16[3,2,128,256]{3,2,1,0:T(8,128)(2,1)S(1)}, u32[]{:S(2)}, u32[]{:S(2)}) collective-permute-start(bf16[3,2,128,256]{3,2,1,0:T(8,128)(2,1)S(1)} %get-tuple-element.154), channel_id=1, source_target_pairs={{0,4},{4,0},{8,12},{12,8},{16,20},{20,16},{24,28},{28,24},{1,5},{5... | collective-permute-start | bytes 1179656 | tf_op jit(solution)/shard_map/ppermute | solution.py:66
  105.8 29.9 %collective-permute-start.21 = (bf16[3,2,128,256]{3,2,1,0:T(8,128)(2,1)S(1)}, bf16[3,2,128,256]{3,2,1,0:T(8,128)(2,1)S(1)}, u32[]{:S(2)}, u32[]{:S(2)}) collective-permute-start(bf16[3,2,128,256]{3,2,1,0:T(8,128)(2,1)S(1)} %get-tuple-element.155), channel_id=1, source_target_pairs={{0,8},{4,12},{8,0},{12,4},{16,24},{20,28},{24,16},{28,20},{1,9},{5... | collective-permute-start | bytes 1179656 | tf_op jit(solution)/shard_map/ppermute | solution.py:66
  107.4 34.4 %collective-permute-start.22 = (bf16[3,2,128,256]{3,2,1,0:T(8,128)(2,1)S(1)}, bf16[3,2,128,256]{3,2,1,0:T(8,128)(2,1)S(1)}, u32[]{:S(2)}, u32[]{:S(2)}) collective-permute-start(bf16[3,2,128,256]{3,2,1,0:T(8,128)(2,1)S(1)} %get-tuple-element.156), channel_id=1, source_target_pairs={{0,12},{4,8},{8,4},{12,0},{16,28},{20,24},{24,20},{28,16},{1,13},{... | collective-permute-start | bytes 1179656 | tf_op jit(solution)/shard_map/ppermute | solution.py:66
  135.7 22.0 %copy-start.7 = (bf16[3,2,128,256]{3,2,1,0:T(8,128)(2,1)}, bf16[3,2,128,256]{3,2,1,0:T(8,128)(2,1)S(1)}, u32[]{:S(2)}) copy-start(bf16[3,2,128,256]{3,2,1,0:T(8,128)(2,1)S(1)} %collective-permute-done.20.refs_5_) | copy-start | bytes 1179652
  135.7 22.0 %copy-start.8 = (bf16[3,2,128,256]{3,2,1,0:T(8,128)(2,1)}, bf16[3,2,128,256]{3,2,1,0:T(8,128)(2,1)S(1)}, u32[]{:S(2)}) copy-start(bf16[3,2,128,256]{3,2,1,0:T(8,128)(2,1)S(1)} %collective-permute-done.21.refs_7_) | copy-start | bytes 1179652
  141.8 15.9 %copy-start.9 = (bf16[3,2,128,256]{3,2,1,0:T(8,128)(2,1)}, bf16[3,2,128,256]{3,2,1,0:T(8,128)(2,1)S(1)}, u32[]{:S(2)}) copy-start(bf16[3,2,128,256]{3,2,1,0:T(8,128)(2,1)S(1)} %collective-permute-done.22.refs_9_) | copy-start | bytes 1179652
  141.8 7.4 %collective-permute-start.23 = (bf16[2,256,1024]{2,1,0:T(8,128)(2,1)S(1)}, bf16[2,256,1024]{2,1,0:T(8,128)(2,1)S(1)}, u32[]{:S(2)}, u32[]{:S(2)}) collective-permute-start(bf16[2,256,1024]{2,1,0:T(8,128)(2,1)S(1)} %collective-permute-done.16.refs_2_), channel_id=1, source_target_pairs={{0,1},{1,0},{2,3},{3,2},{4,5},{5,4},{6,7},{7,6},{8,9},{9,8},{10,11... | collective-permute-start | bytes 3145736 | tf_op jit(solution)/shard_map/ppermute | solution.py:66
  144.9 0.8 copy-start.4
  145.7 12.0 %collective-permute-start.24 = (bf16[3,2,128,256]{3,2,1,0:T(8,128)(2,1)S(1)}, bf16[3,2,128,256]{3,2,1,0:T(8,128)(2,1)S(1)}, u32[]{:S(2)}, u32[]{:S(2)}) collective-permute-start(bf16[3,2,128,256]{3,2,1,0:T(8,128)(2,1)S(1)} %get-tuple-element.175), channel_id=1, source_target_pairs={{0,4},{4,0},{8,12},{12,8},{16,20},{20,16},{24,28},{28,24},{1,5},{5... | collective-permute-start | bytes 1179656 | tf_op jit(solution)/shard_map/ppermute | solution.py:66
  146.8 11.9 %collective-permute-start.25 = (bf16[3,2,128,256]{3,2,1,0:T(8,128)(2,1)S(1)}, bf16[3,2,128,256]{3,2,1,0:T(8,128)(2,1)S(1)}, u32[]{:S(2)}, u32[]{:S(2)}) collective-permute-start(bf16[3,2,128,256]{3,2,1,0:T(8,128)(2,1)S(1)} %get-tuple-element.177), channel_id=1, source_target_pairs={{0,8},{4,12},{8,0},{12,4},{16,24},{20,28},{24,16},{28,20},{1,9},{5... | collective-permute-start | bytes 1179656 | tf_op jit(solution)/shard_map/ppermute | solution.py:66
  146.8 20.1 %collective-permute-start.26 = (bf16[3,2,128,256]{3,2,1,0:T(8,128)(2,1)S(1)}, bf16[3,2,128,256]{3,2,1,0:T(8,128)(2,1)S(1)}, u32[]{:S(2)}, u32[]{:S(2)}) collective-permute-start(bf16[3,2,128,256]{3,2,1,0:T(8,128)(2,1)S(1)} %get-tuple-element.179), channel_id=1, source_target_pairs={{0,12},{4,8},{8,4},{12,0},{16,28},{20,24},{24,20},{28,16},{1,13},{... | collective-permute-start | bytes 1179656 | tf_op jit(solution)/shard_map/ppermute | solution.py:66
  157.7 9.2 %copy-start.10 = (bf16[3,2,128,256]{3,2,1,0:T(8,128)(2,1)}, bf16[3,2,128,256]{3,2,1,0:T(8,128)(2,1)S(1)}, u32[]{:S(2)}) copy-start(bf16[3,2,128,256]{3,2,1,0:T(8,128)(2,1)S(1)} %collective-permute-done.24.refs_6_) | copy-start | bytes 1179652
  158.8 8.1 %copy-start.11 = (bf16[3,2,128,256]{3,2,1,0:T(8,128)(2,1)}, bf16[3,2,128,256]{3,2,1,0:T(8,128)(2,1)S(1)}, u32[]{:S(2)}) copy-start(bf16[3,2,128,256]{3,2,1,0:T(8,128)(2,1)S(1)} %collective-permute-done.25.refs_8_) | copy-start | bytes 1179652
  166.9 0.7 copy-start.12

commit v3 on v1

v3 whole, which is shorter than its diff:
```python
import functools

import jax
import jax.numpy as jnp
import numpy as np
from jax import lax
from jax.experimental import pallas as pl
from jax.experimental.pallas import tpu as pltpu
from jax.sharding import PartitionSpec as P

step_size = 0.5
highest_total = 4
row_tile = 16
pieces = 2
MIB = 1024 * 1024
f32 = jnp.float32
bf16 = jnp.bfloat16


def index_rows(slots, modes):
    entries = [()]
    for _ in range(modes):
        entries = [
            entry + (level,)
            for entry in entries
            for level in range(highest_total + 1)
            if sum(entry) + level <= highest_total
        ]
    return sorted(entries, key=lambda entry: (sum(entry), entry))[:slots]


def coupled_to(rows):
    lookup = {entry: place for place, entry in enumerate(rows)}
    result = []
    for entry in rows:
        terms = []
        for mode, level in enumerate(entry):
            raised = entry[:mode] + (level + 1,) + entry[mode + 1 :]
            if raised in lookup:
                terms.append((lookup[raised], mode, True, 1))
            if level > 0:
                lowered = entry[:mode] + (level - 1,) + entry[mode + 1 :]
                terms.append((lookup[lowered], mode, False, level))
        result.append(terms)
    return result


def smaller_class(rows):
    classes = [[c for c, entry in enumerate(rows) if sum(entry) % 2 == rest] for rest in (0, 1)]
    return min(classes, key=len)


def params(megabytes):
    return pltpu.CompilerParams(vmem_limit_bytes=megabytes * MIB)


def whole():
    return pl.BlockSpec(memory_space=pltpu.VMEM)


def anywhere():
    return pl.BlockSpec(memory_space=pl.ANY)


def scalars():
    return pl.BlockSpec(memory_space=pltpu.SMEM)


def swap(array, axis, size, bit):
    return lax.ppermute(array, axis, [(i, i ^ bit) for i in range(size)])


def tie(arrays):
    return lax.optimization_barrier(arrays)


def row_bits(size):
    return [1 << i for i in reversed(range(size.bit_length() - 1))]


def tree(array, size, bits):
    parts = {0: array}
    for bit in bits:
        for mask in list(parts):
            parts[mask ^ bit] = swap(parts[mask], "row", size, bit)
    return parts


def section_kernel(where, state, slope, section, *chunks):
    value = (state[...].astype(f32) + (0.5 * step_size) * slope[...]).astype(bf16)
    section[...] = value
    width = chunks[0].shape[-1]
    for b, chunk in enumerate(chunks):
        columns = pl.ds(pl.multiple_of((where[0] ^ b) * width, 128), width)
        chunk[...] = section[:, :, :, columns]


def make_section(p, split, state, prev_slope, place, group):
    ops, parts, rows, columns = state.shape
    height, width = rows // split, columns // group
    block = pl.BlockSpec((1, parts, height, columns), lambda a, _: (a, 0, p, 0))
    out = pl.BlockSpec((1, parts, height, columns), lambda a, _: (a, 0, 0, 0))
    chunk = pl.BlockSpec((1, parts, height, width), lambda a, _: (a, 0, 0, 0))
    section, *chunks = pl.pallas_call(
        section_kernel,
        grid_spec=pltpu.PrefetchScalarGridSpec(
            num_scalar_prefetch=1,
            grid=(ops,),
            in_specs=[block, block],
            out_specs=[out] + [chunk] * group,
        ),
        out_shape=[jax.ShapeDtypeStruct((ops, parts, height, columns), bf16)]
        + [jax.ShapeDtypeStruct((ops, parts, height, width), bf16)] * group,
        compiler_params=params(56),
        cost_estimate=pl.CostEstimate(flops=1, bytes_accessed=1, transcendentals=0),
        name="section",
    )(place, state, prev_slope)
    return section, chunks


def fill_factors(vrows, vcols, coupling, factors):
    modes = vrows.shape[0]
    for k in range(modes):
        first = vrows[k]
        second = vcols[k : k + 1, :]
        diff = first - second
        factors[k] = diff
        factors[modes + k] = coupling[0, k] * diff
        factors[2 * modes + k] = coupling[1, k] * (first + second)


def add_terms(terms, places, held, factors, modes, rows, real, imag):
    for other, mode, child, count in terms:
        place = places[other]
        x_real = held[place, 0, rows, :].astype(f32)
        x_imag = held[place, 1, rows, :].astype(f32)
        if child:
            diff = factors[mode, rows, :]
            real = real + diff * x_imag
            imag = imag - diff * x_real
        else:
            first = factors[modes + mode, rows, :]
            second = factors[2 * modes + mode, rows, :]
            if count != 1:
                first, second = count * first, count * second
            real = real + (first * x_imag + second * x_real)
            imag = imag + (second * x_imag - first * x_real)
    return real, imag


def partial_kernel(links, sides, group, places, coupling, vrows, vcols, *refs):
    chunks, out, held, factors, sems = refs[:group], *refs[group:]
    modes = vrows.shape[0]
    height, width = held.shape[2:]
    ops = chunks[0].shape[0]
    empty = group * ops
    loads = [
        pltpu.make_async_copy(chunk, held.at[pl.ds(b * ops, ops)], sems.at[b])
        for b, chunk in enumerate(chunks)
    ]
    for load in loads:
        load.start()
    fill_factors(vrows, vcols, coupling, factors)
    held[empty] = jnp.zeros(held.shape[1:], bf16)
    for load in loads:
        load.wait()
    for u, c in enumerate(sides):

        @pl.when(places[c] < empty)
        def _():
            out[u] = held[places[c]]

        @pl.when(places[c] == empty)
        def _():
            @pl.loop(0, height // row_tile)
            def _(i):
                rows = pl.ds(pl.multiple_of(i * row_tile, row_tile), row_tile)
                zero = jnp.zeros((row_tile, width), f32)
                real, imag = add_terms(links[c], places, held, factors, modes, rows, zero, zero)
                out[u, 0, rows, :] = real.astype(bf16)
                out[u, 1, rows, :] = imag.astype(bf16)


def coupled_kernel(links, sides, group, places, coupling, vrows, vcols, *refs):
    chunks, received, outs = refs[:group], refs[group], refs[group + 1 : 2 * group + 1]
    held, done, factors, spots, sems = refs[2 * group + 1 :]
    modes = vrows.shape[0]
    height, width = held.shape[2:]
    ops = chunks[0].shape[0]
    empty = group * ops
    loads = [
        pltpu.make_async_copy(chunk, held.at[pl.ds(b * ops, ops)], sems.at[b])
        for b, chunk in enumerate(chunks)
    ]
    loads.append(
        pltpu.make_async_copy(received, held.at[pl.ds(empty + 1, len(sides))], sems.at[group])
    )
    for load in loads:
        load.start()
    fill_factors(vrows, vcols, coupling, factors)
    held[empty] = jnp.zeros(held.shape[1:], bf16)
    for c in range(len(links)):
        spots[c] = places[c]
    for u, c in enumerate(sides):
        spots[c] = jnp.where(places[c] == empty, empty + 1 + u, places[c])
    for load in loads:
        load.wait()
    for c in range(len(links)):

        @pl.when(places[c] < empty)
        def _():
            @pl.loop(0, height // row_tile)
            def _(i):
                rows = pl.ds(pl.multiple_of(i * row_tile, row_tile), row_tile)
                if c in sides:
                    u = empty + 1 + sides.index(c)
                    real, imag = held[u, 0, rows, :].astype(f32), held[u, 1, rows, :].astype(f32)
                else:
                    real = imag = jnp.zeros((row_tile, width), f32)
                real, imag = add_terms(links[c], spots, held, factors, modes, rows, real, imag)
                done[places[c], 0, rows, :] = real.astype(bf16)
                done[places[c], 1, rows, :] = imag.astype(bf16)

    stores = [
        pltpu.make_async_copy(done.at[pl.ds(b * ops, ops)], out, sems.at[group + 1 + b])
        for b, out in enumerate(outs)
    ]
    for store in stores:
        store.start()
    for store in stores:
        store.wait()


def coupling_scratch(entries, height, width, modes):
    return [pltpu.VMEM((entries, 2, height, width), bf16)], [pltpu.VMEM((3 * modes, height, width), f32)]


def make_partial(chunks, places, coupling, vrows, vcols, links, sides):
    group = len(chunks)
    ops, _, height, width = chunks[0].shape
    held, factors = coupling_scratch(group * ops + 1, height, width, vrows.shape[0])
    size = height * width
    return pl.pallas_call(
        functools.partial(partial_kernel, links, sides, group),
        in_specs=[scalars(), scalars()] + [whole()] * 2 + [anywhere()] * group,
        out_specs=whole(),
        out_shape=jax.ShapeDtypeStruct((len(sides), 2, height, width), bf16),
        scratch_shapes=held + factors + [pltpu.SemaphoreType.DMA((group,))],
        compiler_params=params(32),
        cost_estimate=pl.CostEstimate(
            flops=40 * len(sides) * size,
            bytes_accessed=4 * size * (group * ops + len(sides)),
            transcendentals=0,
        ),
        name="partial_sums",
    )(places, coupling, vrows, vcols, *chunks)


def make_coupled(chunks, received, places, coupling, vrows, vcols, links, sides):
    group = len(chunks)
    ops, _, height, width = chunks[0].shape
    held, factors = coupling_scratch(group * ops + 1 + len(sides), height, width, vrows.shape[0])
    size = height * width
    return pl.pallas_call(
        functools.partial(coupled_kernel, links, sides, group),
        in_specs=[scalars(), scalars()] + [whole()] * 2 + [anywhere()] * (1 + group),
        out_specs=[anywhere()] * group,
        out_shape=[jax.ShapeDtypeStruct(chunks[0].shape, bf16)] * group,
        scratch_shapes=held
        + [pltpu.VMEM((group * ops, 2, height, width), bf16)]
        + factors
        + [pltpu.SMEM((len(links),), jnp.int32), pltpu.SemaphoreType.DMA((2 * group + 1,))],
        compiler_params=params(32),
        cost_estimate=pl.CostEstimate(
            flops=40 * group * ops * size,
            bytes_accessed=4 * size * (2 * group * ops + len(sides)),
            transcendentals=0,
        ),
        name="coupling_sums",
    )(places, coupling, vrows, vcols, *chunks, received)


def complex_rows(left, right):
    _, height, depth = left.shape
    left = left.reshape(2 * height, depth)
    first = jnp.dot(left, right[0], preferred_element_type=f32)
    second = jnp.dot(left, right[1], preferred_element_type=f32)
    return first[:height] - second[height:], second[:height] + first[height:]


def right_kernel(split, count, where, decay, *refs):
    sections, h_parts, (out, h_all) = refs[:split], refs[split:-2], refs[-2:]
    j, a = pl.program_id(0), pl.program_id(1)
    rows, tile = h_parts[0].shape[1:]
    height = sections[0].shape[2]

    @pl.when(a == 0)
    def _():
        for b in range(count):
            place = pl.ds(pl.multiple_of((where[0] ^ b) * rows, row_tile), rows)
            h_all[:, place, :] = h_parts[b][...]

    columns = pl.ds(pl.multiple_of(j * tile, 128), tile)
    lost = decay[a]
    for p, section in enumerate(sections):
        real, imag = complex_rows(section[a], h_all)
        here = slice(p * height, (p + 1) * height)
        out[0, 0, here, :] = -imag - lost * section[a, 0, :, columns].astype(f32)
        out[0, 1, here, :] = real - lost * section[a, 1, :, columns].astype(f32)


def make_right(sections, h_parts, place, decay):
    ops, _, height, columns = sections[0].shape
    split, count = len(sections), len(h_parts)
    rows, tile = height * split, min(columns, 256)
    held = pl.BlockSpec((ops, 2, height, columns), lambda j, a: (0, 0, 0, 0))
    return pl.pallas_call(
        functools.partial(right_kernel, split, count),
        grid=(columns // tile, ops),
        in_specs=[scalars(), scalars()]
        + [held] * split
        + [pl.BlockSpec((2, rows, tile), lambda j, a: (0, 0, j))] * count,
        out_specs=pl.BlockSpec((1, 2, rows, tile), lambda j, a: (a, 0, 0, j)),
        out_shape=jax.ShapeDtypeStruct((ops, 2, rows, columns), f32),
        scratch_shapes=[pltpu.VMEM((2, count * rows, tile), bf16)],
        compiler_params=params(40),
        cost_estimate=pl.CostEstimate(
            flops=8 * ops * rows * columns * columns,
            bytes_accessed=4 * columns * (columns + 3 * ops * rows),
            transcendentals=0,
        ),
        name="right_products",
    )(place, decay, *sections, *h_parts)


def left_kernel(count, where, h_own, base, *refs):
    s_parts, (out, s_all) = refs[:count], refs[count:]
    height = s_parts[0].shape[2]
    for b in range(count):
        place = pl.ds(pl.multiple_of((where[0] ^ b) * height, row_tile), height)
        s_all[:, place, :] = s_parts[b][0]
    real, imag = complex_rows(h_own[...], s_all)
    out[0, 0] = base[0, 0] + imag
    out[0, 1] = base[0, 1] - real


def make_left(s_parts, h_columns, base, place):
    ops, _, height, columns = s_parts[0].shape
    count, rows, tile = len(s_parts), base.shape[2], min(columns, 256)
    block = pl.BlockSpec((1, 2, rows, tile), lambda j, a: (a, 0, 0, j))
    return pl.pallas_call(
        functools.partial(left_kernel, count),
        grid=(columns // tile, ops),
        in_specs=[
            scalars(),
            pl.BlockSpec(h_columns.shape, lambda j, a: (0, 0, 0)),
            block,
        ]
        + [pl.BlockSpec((1, 2, height, tile), lambda j, a: (a, 0, 0, j))] * count,
        out_specs=block,
        out_shape=jax.ShapeDtypeStruct(base.shape, f32),
        scratch_shapes=[pltpu.VMEM((2, count * height, tile), bf16)],
        compiler_params=params(40),
        cost_estimate=pl.CostEstimate(
            flops=8 * ops * rows * columns * count * height,
            bytes_accessed=4 * ops * columns * (count * height + 4 * rows),
            transcendentals=0,
        ),
        name="left_products",
    )(place, h_columns, base, *s_parts)


def final_kernel(group, where, product, accumulated, *refs):
    sums, (slope, total) = refs[:group], refs[-2:]
    a, i = pl.program_id(0), pl.program_id(1)
    height, width = slope.shape[2], sums[0].shape[3]
    rows = pl.ds(pl.multiple_of(i * height, row_tile), height)
    for b in range(group):
        columns = pl.ds(pl.multiple_of((where[0] ^ b) * width, 128), width)
        value = product[0, :, :, columns] + sums[b][a, :, rows, :].astype(f32)
        slope[0, :, :, columns] = value
        total[0, :, :, columns] = accumulated[0, :, :, columns] + (step_size / 3.0) * value


def make_final(p, split, product, accumulated, sums, place, earlier=()):
    ops, parts, rows, columns = product.shape
    group, steps = len(sums), 2
    height = rows // split // steps
    block = pl.BlockSpec((1, parts, height, columns), lambda a, i, _: (a, 0, p * steps + i, 0))
    held = pl.BlockSpec(sums[0].shape, lambda a, i, _: (0, 0, 0, 0))
    return pl.pallas_call(
        functools.partial(final_kernel, group),
        grid_spec=pltpu.PrefetchScalarGridSpec(
            num_scalar_prefetch=1,
            grid=(ops, steps),
            in_specs=[block, block] + [held] * group + [anywhere()] * len(earlier),
            out_specs=[block, block],
        ),
        out_shape=[jax.ShapeDtypeStruct(product.shape, f32)] * 2,
        input_output_aliases={3 + group + k: k for k in range(len(earlier))},
        compiler_params=params(56),
        cost_estimate=pl.CostEstimate(
            flops=4 * product.size // split,
            bytes_accessed=18 * product.size // split,
            transcendentals=0,
        ),
        name="outputs",
    )(place, product, accumulated, *sums, *earlier)


def shards(
    hier,
    row,
    state,
    prev_slope,
    accumulated,
    hamiltonian,
    couple_v,
    coupling,
    damping,
    occupation,
    parents,
    children,
):
    ops, _, rows, columns = state.shape
    modes = occupation.shape[1]
    group = hier // 2
    width = columns // group
    split = pieces
    height = rows // split
    table = index_rows(hier * ops, modes)
    links, sides = coupled_to(table), smaller_class(table)

    hier_at, row_at = lax.axis_index("hier"), lax.axis_index("row")
    own = hier_at % group
    own_place, row_place = own.reshape(1).astype(jnp.int32), row_at.reshape(1).astype(jnp.int32)

    bits = row_bits(row)
    top, low = bits[0], bits[1:]

    def spread(p):
        return [chunks[p][0]] + [swap(chunks[p][b], "hier", hier, b) for b in range(1, group)]

    def partial(p):
        return make_partial(got[p], places, coupling, heres[p], vcols, links, sides)

    def coupled(p):
        return make_coupled(got[p], received[p], places, coupling, heres[p], vcols, links, sides)

    def gather_back(done):
        return [done[0]] + [swap(done[b], "hier", hier, b) for b in range(1, group)]

    def joined(near, across):
        far = {mask ^ top: part for mask, part in tree(across, row, low).items()}
        parts = {**near, **far}
        return [parts[b] for b in range(row)]

    got, sent, received, sums, outs = [], [], [], [], []

    half = [occupation] + [swap(occupation, "hier", hier, b) for b in range(1, group)]
    first, first_chunks = make_section(0, split, state, prev_slope, own_place, group)
    first, first_chunks, half, state, prev_slope, couple_v, hamiltonian = tie(
        (first, first_chunks, half, state, prev_slope, couple_v, hamiltonian)
    )

    h_top, h_near = swap(hamiltonian, "row", row, top), tree(hamiltonian, row, low)
    second, second_chunks = make_section(1, split, state, prev_slope, own_place, group)
    chunks, sections = [first_chunks, second_chunks], [first, second]
    got.append(spread(0))

    known = jnp.asarray(np.array(table, np.int32))
    found = jnp.concatenate(half, axis=0)
    same = jnp.all(found[None, :, :] == known[:, None, :], axis=2)
    spot = jnp.arange(group * ops, dtype=jnp.int32)[None, :]
    places = jnp.min(jnp.where(same, spot, group * ops), axis=1).astype(jnp.int32)
    vrows = lax.dynamic_slice_in_dim(couple_v, row_at * rows, rows, 1)[:, :, None]
    vcols = lax.dynamic_slice_in_dim(couple_v, own * width, width, 1)
    heres = [vrows[:, p * height : (p + 1) * height] for p in range(split)]
    decay = jnp.sum(occupation.astype(f32) * damping[None, :], axis=1)
    blocks = hamiltonian.reshape(2, rows, row, split, height)
    h_columns = [blocks[:, :, :, p].reshape(2, rows, row * height) for p in range(split)]
    got, chunks, sections, places, heres, vcols, decay, h_columns, h_top, h_near = tie(
        (got, chunks, sections, places, heres, vcols, decay, h_columns, h_top, h_near)
    )

    sent.append(partial(0))
    received.append(swap(sent[0], "hier", hier, group))
    got.append(spread(1))
    across = swap(sections[0], "row", row, top)
    got, received, across, sections, h_top, h_near = tie(
        (got, received, across, sections, h_top, h_near)
    )

    sent.append(partial(1))
    received.append(swap(sent[1], "hier", hier, group))
    last_across = swap(sections[1], "row", row, top)
    s_parts = joined(tree(sections[0], row, low), across)
    h_parts = joined(h_near, h_top)
    done, s_parts, h_parts = tie((coupled(0), s_parts, h_parts))
    sums.append(gather_back(done))
    base = make_right(sections, h_parts, row_place, decay)
    base = make_left(s_parts, h_columns[0], base, row_place)
    received, last_across, sums, base, sections = tie(
        (received, last_across, sums, base, sections)
    )

    s_parts = joined(tree(sections[1], row, low), last_across)
    sums.append(gather_back(coupled(1)))
    base = make_left(s_parts, h_columns[1], base, row_place)
    for p in range(split):
        outs = make_final(p, split, base, accumulated, sums[p], own_place, outs)
    slope, total = outs
    return slope, total


def solution(mesh):
    return jax.shard_map(
        functools.partial(shards, mesh.shape["hier"], mesh.shape["row"]),
        mesh=mesh,
        in_specs=(
            P("hier", None, "row", None),
            P("hier", None, "row", None),
            P("hier", None, "row", None),
            P(None, "row", None),
            P(),
            P(),
            P(),
            P("hier", None),
            P("hier", None),
            P("hier", None),
        ),
        out_specs=(P("hier", None, "row", None), P("hier", None, "row", None)),
        check_vma=False,
    )
```

time: 250 us -> 171 us (0.68)
  waiting for transfers between devices: 128 us -> 39.2 us
  blocking collectives: 38.4 us -> 0 us
  Pallas kernels: 44.1 us -> 72.7 us
  local copies, waits for them, and re-layouts: 13.8 us -> 27.4 us
  starting transfers between devices: 21.8 us -> 27.9 us
    ppermute x20 -> x26, waiting for transfers between devices: 128 us -> 39.2 us  [swap(): return lax.ppermute(array, axis, [(i, i ^ bit) for i in range(size)])]
    all_gather x1 -> x0, blocking collectives: 38.4 us -> none  [shards(): everyone = lax.all_gather(occupation, 'hier', axis=0, tiled=True)]
    pallas_call x3 -> x7, Pallas kernels: 31.8 us -> 57.5 us  [the longest x2 20.5 us: make_left(): pl.pallas_call(functools.partial(left_kernel, count), grid=(columns // ti...]
    ppermute x20 -> x26, starting transfers between devices: 21.8 us -> 27.9 us  [swap(): return lax.ppermute(array, axis, [(i, i ^ bit) for i in range(size)])]
    unnamed x18 -> x52, local copies, waits for them, and re-layouts: 11.2 us -> 17.1 us
    slice x1 -> x2, local copies, waits for them, and re-layouts: 1.28 us -> 6.77 us  [the longest x1 6.77 us: shards(): blocks[:, :, :, p].reshape(2, rows, row * height)]
    pallas_call x2, Pallas kernels: 6.94 us -> 9.6 us  [make_coupled(): pl.pallas_call(functools.partial(coupled_kernel, links, sides, group), in...]
  transfers between devices with their start and end apart: 20 -> 26, of which waited for: 8 -> 6; matrix products, arithmetic and copies ran while one was open for 4% -> 7% of each run, Pallas kernels for 13% -> 39%
where the time goes in v3:
time: 171 us; the launch traced here: 169 us
  Pallas kernels  72.7 us (43%)
  waiting for transfers between devices  39.2 us (23%)
  starting transfers between devices  27.9 us (16%)
  local copies, waits for them, and re-layouts  27.4 us (16%)
    ppermute x26, waiting for transfers between devices, swap(): return lax.ppermute(array, axis, [(i, i ^ bit) for i in range(size)])  39.2 us
    ppermute x26, starting transfers between devices, swap(): return lax.ppermute(array, axis, [(i, i ^ bit) for i in range(size)])  27.9 us
    pallas_call x2, Pallas kernels, make_left(): pl.pallas_call(functools.partial(left_kernel, count), grid=(columns // ti...  20.5 us
    unnamed x52, local copies, waits for them, and re-layouts  17.1 us
    pallas_call x2, Pallas kernels, make_final(): pl.pallas_call(functools.partial(final_kernel, group), grid_spec=pltpu.Pr...  14.9 us
    pallas_call x1, Pallas kernels, make_right(): pl.pallas_call(functools.partial(right_kernel, split, count), grid=(colum...  12 us
    pallas_call x2, Pallas kernels, make_section(): pl.pallas_call(section_kernel, grid_spec=pltpu.PrefetchScalarGridSpec(num...  10.1 us
    pallas_call x2, Pallas kernels, make_coupled(): pl.pallas_call(functools.partial(coupled_kernel, links, sides, group), in...  9.6 us
  transfers between devices with their start and end apart: 26, of which 6 were waited for; matrix products, arithmetic and copies ran while one was open for 7% of the time, Pallas kernels for 39%

profile of v3, /device:TPU:0, one launch (start us, length us, event | category | flops | bytes accessed | tf_op | source)
XLA Modules:
  0.0 169.2 jit_solution(7757499265144874924)
XLA Ops:
  0.6 4.0 %collective-permute-start.2 = (s32[3,6]{1,0:T(4,128)}, s32[3,6]{1,0:T(4,128)S(1)}, u32[]{:S(2)}, u32[]{:S(2)}) collective-permute-start(s32[3,6]{1,0:T(4,128)} %param.18), channel_id=1, source_target_pairs={{0,12},{4,8},{8,4},{12,0},{16,28},{20,24},{24,20},{28,16},{1,13},{... | collective-permute-start | bytes 224 | tf_op jit(solution)/shard_map/ppermute | solution.py:70
  4.7 0.4 collective-permute-start.1
  5.1 0.2 collective-permute-start
  5.3 0.8 multiply_reduce_fusion.decay
  6.1 5.0 %section.2 = (bf16[3,2,128,1024]{3,2,1,0:T(8,128)(2,1)}, bf16[3,2,128,256]{3,2,1,0:T(8,128)(2,1)}, bf16[3,2,128,256]{3,2,1,0:T(8,128)(2,1)}, bf16[3,2,128,256]{3,2,1,0:T(8,128)(2,1)}, bf16[3,2,128,256]{3,2,1,0:T(8,128)(2,1)}) custom-call(s32[1]{0:T(128)} %bitcast.where, bf16[3,2,256,1024]{3,2,1,0:T(8,128)(2,1)} %state.2, f32[3,2,256,1024]{3,2,1,0:T(8,128)} %slope.2), custom_call_target="tpu_custom_call" | custom-call | flops 1 | bytes 1 | tf_op jit(solution)/shard_map/section/pallas_call | solution.py:104
  11.1 0.0 collective-permute-done
  11.2 0.1 collective-permute-start.7
  11.2 1.9 %collective-permute-start.6 = (bf16[2,256,1024]{2,1,0:T(8,128)(2,1)}, bf16[2,256,1024]{2,1,0:T(8,128)(2,1)}, u32[]{:S(2)}, u32[]{:S(2)}) collective-permute-start(bf16[2,256,1024]{2,1,0:T(8,128)(2,1)} %refs_2_), channel_id=1, source_target_pairs={{0,2},{1,3},{2,0},{3,1},{4,6},{5,7},{6,4},{7,5},{8,10},{9,11},{10,... | collective-permute-start | bytes 3145736 | tf_op jit(solution)/shard_map/ppermute | solution.py:70
  13.2 1.5 collective-permute-start.3
  14.6 1.6 collective-permute-start.4
  16.2 0.4 collective-permute-start.5
  16.7 1.8 %reshape.18 = bf16[2,256,4,2,128]{4,3,2,1,0:T(2,128)(2,1)S(1)} reshape(bf16[2,256,1024]{2,1,0:T(8,128)(2,1)} %refs_2_) | data formatting | bytes 2097152 | tf_op jit(solution)/shard_map/reshape | solution.py:480
  18.4 6.8 %slice_reduce_fusion = (bf16[2,256,4,128]{3,2,1,0:T(4,128)(2,1)}, bf16[2,256,4,128]{3,2,1,0:T(4,128)(2,1)}) fusion(bf16[2,256,4,2,128]{4,3,2,1,0:T(2,128)(2,1)S(1)} %reshape.18), kind=kLoop, calls=%fused_computation | loop fusion | bytes 2097152 | tf_op jit(solution)/shard_map/slice | solution.py:481
  25.2 5.1 %section.3 = (bf16[3,2,128,1024]{3,2,1,0:T(8,128)(2,1)}, bf16[3,2,128,256]{3,2,1,0:T(8,128)(2,1)}, bf16[3,2,128,256]{3,2,1,0:T(8,128)(2,1)}, bf16[3,2,128,256]{3,2,1,0:T(8,128)(2,1)}, bf16[3,2,128,256]{3,2,1,0:T(8,128)(2,1)}) custom-call(s32[1]{0:T(128)} %bitcast.where, bf16[3,2,256,1024]{3,2,1,0:T(8,128)(2,1)} %state.2, f32[3,2,256,1024]{3,2,1,0:T(8,128)} %slope.2), custom_call_target="tpu_custom_call" | custom-call | flops 1 | bytes 1 | tf_op jit(solution)/shard_map/section/pallas_call | solution.py:104
  30.4 0.2 copy.24.vrows
  30.5 0.2 copy.23.vrows
  30.8 0.2 reshape_squeeze.7.h_own
  31.0 1.2 reshape_squeeze.6.h_own
  32.3 0.1 compare_reduce_fusion
  32.4 1.8 %collective-permute-done.5.refs_3_ = bf16[3,2,128,256]{3,2,1,0:T(8,128)(2,1)S(1)} collective-permute-done((bf16[3,2,128,256]{3,2,1,0:T(8,128)(2,1)}, bf16[3,2,128,256]{3,2,1,0:T(8,128)(2,1)S(1)}, u32[]{:S(2)}, u32[]{:S(2)}) %collective-permute-start.5) | collective-permute-done | bytes 393248 | tf_op jit(solution)/shard_map/ppermute | solution.py:70
  34.2 3.1 %collective-permute-done.6.refs_4_ = bf16[2,256,1024]{2,1,0:T(8,128)(2,1)} collective-permute-done((bf16[2,256,1024]{2,1,0:T(8,128)(2,1)}, bf16[2,256,1024]{2,1,0:T(8,128)(2,1)}, u32[]{:S(2)}, u32[]{:S(2)}) %collective-permute-start.6) | collective-permute-done | bytes 1048608 | tf_op jit(solution)/shard_map/ppermute | solution.py:70
  37.2 1.8 %collective-permute-start.12 = (bf16[3,2,128,1024]{3,2,1,0:T(8,128)(2,1)}, bf16[3,2,128,1024]{3,2,1,0:T(8,128)(2,1)S(1)}, u32[]{:S(2)}, u32[]{:S(2)}) collective-permute-start(bf16[3,2,128,1024]{3,2,1,0:T(8,128)(2,1)} %get-tuple-element.160.refs_0_), channel_id=1, source_target_pairs={{0,2},{1,3},{2,0},{3,1},{4,6},{5,7},{6,4},{7,5},{8,10},{9,11},{10,... | collective-permute-start | bytes 4718600 | tf_op jit(solution)/shard_map/ppermute | solution.py:70
  39.0 2.3 %partial_sums.2 = bf16[6,2,128,256]{3,2,1,0:T(8,128)(2,1)S(1)} custom-call(s32[24]{0:T(128)S(1)} %select_reduce_fusion.places, f32[2,6]{1,0:T(2,128)S(1)} %copy-done.13, f32[6,128,1]{2,1,0:T(8,128)S(1)} %copy.23.vrows, f32[6,256]{1,0:T(8,128)S(1)} %get-tuple-element.124.vcols, bf16[3,2,128,256]{3,2,1,0:T(8,128)(2,1)S(1)} %copy-done.5, ...), custom_call_target="tpu_custom_call" | custom-call | flops 7864320 | bytes 2359296 | tf_op jit(solution)/shard_map/partial_sums/pallas_call | solution.py:243
  41.3 2.7 %collective-permute-start.11 = (bf16[6,2,128,256]{3,2,1,0:T(8,128)(2,1)S(1)}, bf16[6,2,128,256]{3,2,1,0:T(8,128)(2,1)S(1)}, u32[]{:S(2)}, u32[]{:S(2)}) collective-permute-start(bf16[6,2,128,256]{3,2,1,0:T(8,128)(2,1)S(1)} %partial_sums.2), channel_id=1, source_target_pairs={{0,16},{4,20},{8,24},{12,28},{16,0},{20,4},{24,8},{28,12},{1,17},{... | collective-permute-start | bytes 2359304 | tf_op jit(solution)/shard_map/ppermute | solution.py:70
  44.1 1.5 collective-permute-start.8
  45.6 1.6 collective-permute-start.9
  47.2 0.4 collective-permute-start.10
  47.6 7.9 %collective-permute-done.8.refs_1_ = bf16[3,2,128,256]{3,2,1,0:T(8,128)(2,1)S(1)} collective-permute-done((bf16[3,2,128,256]{3,2,1,0:T(8,128)(2,1)}, bf16[3,2,128,256]{3,2,1,0:T(8,128)(2,1)S(1)}, u32[]{:S(2)}, u32[]{:S(2)}) %collective-permute-start.8) | collective-permute-done | bytes 393248 | tf_op jit(solution)/shard_map/ppermute | solution.py:70
  55.4 15.2 %collective-permute-done.9.refs_2_ = bf16[3,2,128,256]{3,2,1,0:T(8,128)(2,1)S(1)} collective-permute-done((bf16[3,2,128,256]{3,2,1,0:T(8,128)(2,1)}, bf16[3,2,128,256]{3,2,1,0:T(8,128)(2,1)S(1)}, u32[]{:S(2)}, u32[]{:S(2)}) %collective-permute-start.9) | collective-permute-done | bytes 393248 | tf_op jit(solution)/shard_map/ppermute | solution.py:70
  70.7 9.1 %collective-permute-done.10.refs_3_ = bf16[3,2,128,256]{3,2,1,0:T(8,128)(2,1)S(1)} collective-permute-done((bf16[3,2,128,256]{3,2,1,0:T(8,128)(2,1)}, bf16[3,2,128,256]{3,2,1,0:T(8,128)(2,1)S(1)}, u32[]{:S(2)}, u32[]{:S(2)}) %collective-permute-start.10) | collective-permute-done | bytes 393248 | tf_op jit(solution)/shard_map/ppermute | solution.py:70
  79.8 0.5 collective-permute-start.15
  80.3 0.1 collective-permute-start.17
  80.3 0.5 collective-permute-start.14
  80.9 1.0 copy-done.3
  81.8 3.2 %partial_sums.3 = bf16[6,2,128,256]{3,2,1,0:T(8,128)(2,1)} custom-call(s32[24]{0:T(128)S(1)} %select_reduce_fusion.places, f32[2,6]{1,0:T(2,128)S(1)} %copy-done.13, f32[6,128,1]{2,1,0:T(8,128)S(1)} %copy.24.vrows, f32[6,256]{1,0:T(8,128)S(1)} %get-tuple-element.124.vcols, bf16[3,2,128,256]{3,2,1,0:T(8,128)(2,1)S(1)} %copy-done.3, ...), custom_call_target="tpu_custom_call" | custom-call | flops 7864320 | bytes 2359296 | tf_op jit(solution)/shard_map/partial_sums/pallas_call | solution.py:243
  85.1 1.0 collective-permute-start.13
  86.1 5.0 %coupling_sums.2 = (bf16[3,2,128,256]{3,2,1,0:T(8,128)(2,1)S(1)}, bf16[3,2,128,256]{3,2,1,0:T(8,128)(2,1)}, bf16[3,2,128,256]{3,2,1,0:T(8,128)(2,1)}, bf16[3,2,128,256]{3,2,1,0:T(8,128)(2,1)}) custom-call(s32[24]{0:T(128)S(1)} %select_reduce_fusion.places, f32[2,6]{1,0:T(2,128)S(1)} %copy-done.13, f32[6,128,1]{2,1,0:T(8,128)S(1)} %copy.23.vrows, ...), custom_call_target="tpu_custom_call" | custom-call | flops 15728640 | bytes 3932160 | tf_op jit(solution)/shard_map/coupling_sums/pallas_call | solution.py:264
  91.1 0.7 copy-done.11
  91.9 1.0 copy-done.14
  92.8 1.2 copy-done.9
  94.0 0.6 collective-permute-start.18
  94.6 3.1 %collective-permute-start.19 = (bf16[3,2,128,256]{3,2,1,0:T(8,128)(2,1)}, bf16[3,2,128,256]{3,2,1,0:T(8,128)(2,1)S(1)}, u32[]{:S(2)}, u32[]{:S(2)}) collective-permute-start(bf16[3,2,128,256]{3,2,1,0:T(8,128)(2,1)} %get-tuple-element.152), channel_id=1, source_target_pairs={{0,8},{4,12},{8,0},{12,4},{16,24},{20,28},{24,16},{28,20},{1,9},{5... | collective-permute-start | bytes 1179656 | tf_op jit(solution)/shard_map/ppermute | solution.py:70
  97.7 1.4 copy-done.7
  99.1 1.2 copy-done.15
  100.3 12.0 %right_products.1.base = f32[3,2,256,1024]{3,2,1,0:T(8,128)S(1)} custom-call(s32[1]{0:T(128)} %bitcast.1.where, f32[3]{0:T(128)S(1)} %multiply_reduce_fusion.decay, bf16[3,2,128,1024]{3,2,1,0:T(8,128)(2,1)S(1)} %copy-done.7, bf16[3,2,128,1024]{3,2,1,0:T(8,128)(2,1)S(1)} %copy-done.6, bf16[2,256,1024]{2,1,0:T(8,128)(2,1)} %refs_2_, ...), custom_call_target="tpu_custom_call" | custom-call | flops 6442450944 | bytes 13631488 | tf_op jit(solution)/shard_map/right_products/pallas_call | solution.py:317
  112.4 0.0 copy-start.2
  112.4 2.7 %copy-done.2 = f32[3,2,256,1024]{3,2,1,0:T(8,128)} copy-done((f32[3,2,256,1024]{3,2,1,0:T(8,128)}, f32[3,2,256,1024]{3,2,1,0:T(8,128)S(1)}, u32[]{:S(2)}) %copy-start.2) | copy-done | bytes 6291480
  115.1 1.4 copy-done.10
  116.5 10.3 %left_products.2.base = f32[3,2,256,1024]{3,2,1,0:T(8,128)S(1)} custom-call(s32[1]{0:T(128)} %bitcast.1.where, bf16[2,256,512]{2,1,0:T(8,128)(2,1)S(1)} %reshape_squeeze.6.h_own, f32[3,2,256,1024]{3,2,1,0:T(8,128)} %copy-done.2, bf16[3,2,128,1024]{3,2,1,0:T(8,128)(2,1)S(1)} %copy-done.8, bf16[3,2,128,1024]{3,2,1,0:T(8,128)(2,1)S(1)} %copy-done.10, ...), custom_call_target="tpu_custom_call" | custom-call | flops 3221225472 | bytes 18874368 | tf_op jit(solution)/shard_map/left_products/pallas_call | solution.py:351
  126.8 0.0 copy-start.1
  126.8 2.7 %copy-done.1 = f32[3,2,256,1024]{3,2,1,0:T(8,128)} copy-done((f32[3,2,256,1024]{3,2,1,0:T(8,128)}, f32[3,2,256,1024]{3,2,1,0:T(8,128)S(1)}, u32[]{:S(2)}) %copy-start.1) | copy-done | bytes 6291480
  129.5 2.2 %collective-permute-done.20.refs_3_ = bf16[3,2,128,256]{3,2,1,0:T(8,128)(2,1)S(1)} collective-permute-done((bf16[3,2,128,256]{3,2,1,0:T(8,128)(2,1)}, bf16[3,2,128,256]{3,2,1,0:T(8,128)(2,1)S(1)}, u32[]{:S(2)}, u32[]{:S(2)}) %collective-permute-start.20) | collective-permute-done | bytes 393248 | tf_op jit(solution)/shard_map/ppermute | solution.py:70
  131.7 0.5 collective-permute-start.22
  132.2 4.6 %coupling_sums.3 = (bf16[3,2,128,256]{3,2,1,0:T(8,128)(2,1)S(1)}, bf16[3,2,128,256]{3,2,1,0:T(8,128)(2,1)S(1)}, bf16[3,2,128,256]{3,2,1,0:T(8,128)(2,1)S(1)}, bf16[3,2,128,256]{3,2,1,0:T(8,128)(2,1)S(1)}) custom-call(s32[24]{0:T(128)S(1)} %select_reduce_fusion.places, f32[2,6]{1,0:T(2,128)S(1)} %copy-done.13, f32[6,128,1]{2,1,0:T(8,128)S(1)} %copy.24.vrows, ...), custom_call_target="tpu_custom_call" | custom-call | flops 15728640 | bytes 3932160 | tf_op jit(solution)/shard_map/coupling_sums/pallas_call | solution.py:264
  136.8 1.4 collective-permute-start.23
  138.2 0.1 collective-permute-start.24
  138.2 2.1 %collective-permute-start.25 = (bf16[3,2,128,256]{3,2,1,0:T(8,128)(2,1)S(1)}, bf16[3,2,128,256]{3,2,1,0:T(8,128)(2,1)S(1)}, u32[]{:S(2)}, u32[]{:S(2)}) collective-permute-start(bf16[3,2,128,256]{3,2,1,0:T(8,128)(2,1)S(1)} %get-tuple-element.171), channel_id=1, source_target_pairs={{0,12},{4,8},{8,4},{12,0},{16,28},{20,24},{24,20},{28,16},{1,13},{... | collective-permute-start | bytes 1179656 | tf_op jit(solution)/shard_map/ppermute | solution.py:70
  140.3 10.2 %left_products.3.product = f32[3,2,256,1024]{3,2,1,0:T(8,128)S(1)} custom-call(s32[1]{0:T(128)} %bitcast.1.where, bf16[2,256,512]{2,1,0:T(8,128)(2,1)S(1)} %reshape_squeeze.7.h_own, f32[3,2,256,1024]{3,2,1,0:T(8,128)} %copy-done.1, bf16[3,2,128,1024]{3,2,1,0:T(8,128)(2,1)S(1)} %copy-done.6, bf16[3,2,128,1024]{3,2,1,0:T(8,128)(2,1)S(1)} %collective-permute-done.21.refs_1_, ...), custom_call_target="tpu_custom_call" | custom-call | flops 3221225472 | bytes 18874368 | tf_op jit(solution)/shard_map/left_products/pallas_call | solution.py:351
  150.6 2.7 %copy-done = f32[3,2,256,1024]{3,2,1,0:T(8,128)} copy-done((f32[3,2,256,1024]{3,2,1,0:T(8,128)}, f32[3,2,256,1024]{3,2,1,0:T(8,128)S(1)}, u32[]{:S(2)}) %copy-start) | copy-done | bytes 6291480
  153.3 7.4 %outputs.2 = (f32[3,2,256,1024]{3,2,1,0:T(8,128)}, f32[3,2,256,1024]{3,2,1,0:T(8,128)}) custom-call(s32[1]{0:T(128)} %bitcast.where, f32[3,2,256,1024]{3,2,1,0:T(8,128)} %copy-done, f32[3,2,256,1024]{3,2,1,0:T(8,128)} %accumulated.3, bf16[3,2,128,256]{3,2,1,0:T(8,128)(2,1)} %copy-done.11, bf16[3,2,128,256]{3,2,1,0:T(8,128)(2,1)} %copy-done.17, ...), custom_call_target="tpu_custom_call" | custom-call | flops 3145728 | bytes 14155776 | tf_op jit(solution)/shard_map/outputs/pallas_call | solution.py:391
  160.8 0.7 copy-done.20
  161.5 0.1 copy-done.21
  161.6 0.2 copy-done.22
  161.8 7.4 %outputs.3 = (f32[3,2,256,1024]{3,2,1,0:T(8,128)}, f32[3,2,256,1024]{3,2,1,0:T(8,128)}) custom-call(s32[1]{0:T(128)} %bitcast.where, f32[3,2,256,1024]{3,2,1,0:T(8,128)} %copy-done, f32[3,2,256,1024]{3,2,1,0:T(8,128)} %accumulated.3, bf16[3,2,128,256]{3,2,1,0:T(8,128)(2,1)} %copy-done.12, ...), custom_call_target="tpu_custom_call", output_to_operand_aliasing={{0}: (7, {}), {1}: (8, {})} | custom-call | flops 3145728 | bytes 14155776 | tf_op jit(solution)/shard_map/outputs/pallas_call | solution.py:391
  (63 shorter events, 0.2 us)
Async XLA Ops:
  0.6 16.0 %copy-start.23 = (f32[6,1024]{1,0:T(8,128)S(1)}, f32[6,1024]{1,0:T(8,128)}, u32[]{:S(2)}) copy-start(f32[6,1024]{1,0:T(8,128)} %param.15) | copy-start | bytes 73732
  0.6 10.5 %collective-permute-start.2 = (s32[3,6]{1,0:T(4,128)}, s32[3,6]{1,0:T(4,128)S(1)}, u32[]{:S(2)}, u32[]{:S(2)}) collective-permute-start(s32[3,6]{1,0:T(4,128)} %param.18), channel_id=1, source_target_pairs={{0,12},{4,8},{8,4},{12,0},{16,28},{20,24},{24,20},{28,16},{1,13},{... | collective-permute-start | bytes 224 | tf_op jit(solution)/shard_map/ppermute | solution.py:70
  4.7 6.5 %collective-permute-start.1 = (s32[3,6]{1,0:T(4,128)}, s32[3,6]{1,0:T(4,128)S(1)}, u32[]{:S(2)}, u32[]{:S(2)}) collective-permute-start(s32[3,6]{1,0:T(4,128)} %param.18), channel_id=1, source_target_pairs={{0,8},{4,12},{8,0},{12,4},{16,24},{20,28},{24,16},{28,20},{1,9},{5... | collective-permute-start | bytes 224 | tf_op jit(solution)/shard_map/ppermute | solution.py:70
  5.1 6.0 %collective-permute-start = (s32[3,6]{1,0:T(4,128)}, s32[3,6]{1,0:T(4,128)S(1)}, u32[]{:S(2)}, u32[]{:S(2)}) collective-permute-start(s32[3,6]{1,0:T(4,128)} %param.18), channel_id=1, source_target_pairs={{0,4},{4,0},{8,12},{12,8},{16,20},{20,16},{24,28},{28,24},{1,5},{5... | collective-permute-start | bytes 224 | tf_op jit(solution)/shard_map/ppermute | solution.py:70
  11.2 23.0 %collective-permute-start.7 = (bf16[2,256,1024]{2,1,0:T(8,128)(2,1)}, bf16[2,256,1024]{2,1,0:T(8,128)(2,1)}, u32[]{:S(2)}, u32[]{:S(2)}) collective-permute-start(bf16[2,256,1024]{2,1,0:T(8,128)(2,1)} %refs_2_), channel_id=1, source_target_pairs={{0,1},{1,0},{2,3},{3,2},{4,5},{5,4},{6,7},{7,6},{8,9},{9,8},{10,11... | collective-permute-start | bytes 3145736 | tf_op jit(solution)/shard_map/ppermute | solution.py:70
  11.2 26.0 %collective-permute-start.6 = (bf16[2,256,1024]{2,1,0:T(8,128)(2,1)}, bf16[2,256,1024]{2,1,0:T(8,128)(2,1)}, u32[]{:S(2)}, u32[]{:S(2)}) collective-permute-start(bf16[2,256,1024]{2,1,0:T(8,128)(2,1)} %refs_2_), channel_id=1, source_target_pairs={{0,2},{1,3},{2,0},{3,1},{4,6},{5,7},{6,4},{7,5},{8,10},{9,11},{10,... | collective-permute-start | bytes 3145736 | tf_op jit(solution)/shard_map/ppermute | solution.py:70
  13.2 19.2 %collective-permute-start.3 = (bf16[3,2,128,256]{3,2,1,0:T(8,128)(2,1)}, bf16[3,2,128,256]{3,2,1,0:T(8,128)(2,1)S(1)}, u32[]{:S(2)}, u32[]{:S(2)}) collective-permute-start(bf16[3,2,128,256]{3,2,1,0:T(8,128)(2,1)} %get-tuple-element.96), channel_id=1, source_target_pairs={{0,4},{4,0},{8,12},{12,8},{16,20},{20,16},{24,28},{28,24},{1,5},{5... | collective-permute-start | bytes 1179656 | tf_op jit(solution)/shard_map/ppermute | solution.py:70
  14.6 17.7 %collective-permute-start.4 = (bf16[3,2,128,256]{3,2,1,0:T(8,128)(2,1)}, bf16[3,2,128,256]{3,2,1,0:T(8,128)(2,1)S(1)}, u32[]{:S(2)}, u32[]{:S(2)}) collective-permute-start(bf16[3,2,128,256]{3,2,1,0:T(8,128)(2,1)} %get-tuple-element.97), channel_id=1, source_target_pairs={{0,8},{4,12},{8,0},{12,4},{16,24},{20,28},{24,16},{28,20},{1,9},{5... | collective-permute-start | bytes 1179656 | tf_op jit(solution)/shard_map/ppermute | solution.py:70
  16.2 17.9 %collective-permute-start.5 = (bf16[3,2,128,256]{3,2,1,0:T(8,128)(2,1)}, bf16[3,2,128,256]{3,2,1,0:T(8,128)(2,1)S(1)}, u32[]{:S(2)}, u32[]{:S(2)}) collective-permute-start(bf16[3,2,128,256]{3,2,1,0:T(8,128)(2,1)} %get-tuple-element.98), channel_id=1, source_target_pairs={{0,12},{4,8},{8,4},{12,0},{16,28},{20,24},{24,20},{28,16},{1,13},{... | collective-permute-start | bytes 1179656 | tf_op jit(solution)/shard_map/ppermute | solution.py:70
  25.2 5.5 %copy-start.16 = (bf16[2,256,4,128]{3,2,1,0:T(4,128)(2,1)S(1)}, bf16[2,256,4,128]{3,2,1,0:T(4,128)(2,1)}, u32[]{:S(2)}) copy-start(bf16[2,256,4,128]{3,2,1,0:T(4,128)(2,1)} %get-tuple-element.178) | copy-start | bytes 1572868
  25.2 7.0 %copy-start.24 = (s32[3,6]{1,0:T(4,128)S(1)}, s32[3,6]{1,0:T(4,128)}, u32[]{:S(2)}) copy-start(s32[3,6]{1,0:T(4,128)} %param.18) | copy-start | bytes 220
  25.2 7.0 %copy-start.25 = (s32[24,6]{0,1:T(8,128)S(1)}, s32[24,6]{0,1:T(8,128)}, u32[]{:S(2)}) copy-start(s32[24,6]{0,1:T(8,128)} %constant.37.clone) | copy-start | bytes 1732
  25.2 13.8 %copy-start.5 = (bf16[3,2,128,256]{3,2,1,0:T(8,128)(2,1)S(1)}, bf16[3,2,128,256]{3,2,1,0:T(8,128)(2,1)}, u32[]{:S(2)}) copy-start(bf16[3,2,128,256]{3,2,1,0:T(8,128)(2,1)} %get-tuple-element.137.refs_0_) | copy-start | bytes 1179652
  25.2 13.8 %copy-start.13 = (f32[2,6]{1,0:T(2,128)S(1)}, f32[2,6]{1,0:T(2,128)}, u32[]{:S(2)}) copy-start(f32[2,6]{1,0:T(2,128)} %coupling.7) | copy-start | bytes 148
  32.2 65.5 %copy-start.6 = (bf16[3,2,128,1024]{3,2,1,0:T(8,128)(2,1)S(1)}, bf16[3,2,128,1024]{3,2,1,0:T(8,128)(2,1)}, u32[]{:S(2)}) copy-start(bf16[3,2,128,1024]{3,2,1,0:T(8,128)(2,1)} %get-tuple-element.165.refs_1_.refs_0_) | copy-start | bytes 4718596
  37.2 42.5 %collective-permute-start.12 = (bf16[3,2,128,1024]{3,2,1,0:T(8,128)(2,1)}, bf16[3,2,128,1024]{3,2,1,0:T(8,128)(2,1)S(1)}, u32[]{:S(2)}, u32[]{:S(2)}) collective-permute-start(bf16[3,2,128,1024]{3,2,1,0:T(8,128)(2,1)} %get-tuple-element.160.refs_0_), channel_id=1, source_target_pairs={{0,2},{1,3},{2,0},{3,1},{4,6},{5,7},{6,4},{7,5},{8,10},{9,11},{10,... | collective-permute-start | bytes 4718600 | tf_op jit(solution)/shard_map/ppermute | solution.py:70
  41.3 38.4 %collective-permute-start.11 = (bf16[6,2,128,256]{3,2,1,0:T(8,128)(2,1)S(1)}, bf16[6,2,128,256]{3,2,1,0:T(8,128)(2,1)S(1)}, u32[]{:S(2)}, u32[]{:S(2)}) collective-permute-start(bf16[6,2,128,256]{3,2,1,0:T(8,128)(2,1)S(1)} %partial_sums.2), channel_id=1, source_target_pairs={{0,16},{4,20},{8,24},{12,28},{16,0},{20,4},{24,8},{28,12},{1,17},{... | collective-permute-start | bytes 2359304 | tf_op jit(solution)/shard_map/ppermute | solution.py:70
  44.1 11.4 %collective-permute-start.8 = (bf16[3,2,128,256]{3,2,1,0:T(8,128)(2,1)}, bf16[3,2,128,256]{3,2,1,0:T(8,128)(2,1)S(1)}, u32[]{:S(2)}, u32[]{:S(2)}) collective-permute-start(bf16[3,2,128,256]{3,2,1,0:T(8,128)(2,1)} %get-tuple-element.119), channel_id=1, source_target_pairs={{0,4},{4,0},{8,12},{12,8},{16,20},{20,16},{24,28},{28,24},{1,5},{5... | collective-permute-start | bytes 1179656 | tf_op jit(solution)/shard_map/ppermute | solution.py:70
  45.6 25.1 %collective-permute-start.9 = (bf16[3,2,128,256]{3,2,1,0:T(8,128)(2,1)}, bf16[3,2,128,256]{3,2,1,0:T(8,128)(2,1)S(1)}, u32[]{:S(2)}, u32[]{:S(2)}) collective-permute-start(bf16[3,2,128,256]{3,2,1,0:T(8,128)(2,1)} %get-tuple-element.120), channel_id=1, source_target_pairs={{0,8},{4,12},{8,0},{12,4},{16,24},{20,28},{24,16},{28,20},{1,9},{5... | collective-permute-start | bytes 1179656 | tf_op jit(solution)/shard_map/ppermute | solution.py:70
  47.2 32.6 %collective-permute-start.10 = (bf16[3,2,128,256]{3,2,1,0:T(8,128)(2,1)}, bf16[3,2,128,256]{3,2,1,0:T(8,128)(2,1)S(1)}, u32[]{:S(2)}, u32[]{:S(2)}) collective-permute-start(bf16[3,2,128,256]{3,2,1,0:T(8,128)(2,1)} %get-tuple-element.121), channel_id=1, source_target_pairs={{0,12},{4,8},{8,4},{12,0},{16,28},{20,24},{24,20},{28,16},{1,13},{... | collective-permute-start | bytes 1179656 | tf_op jit(solution)/shard_map/ppermute | solution.py:70
  79.8 13.1 %collective-permute-start.16 = (bf16[3,2,128,1024]{3,2,1,0:T(8,128)(2,1)S(1)}, bf16[3,2,128,1024]{3,2,1,0:T(8,128)(2,1)S(1)}, u32[]{:S(2)}, u32[]{:S(2)}) collective-permute-start(bf16[3,2,128,1024]{3,2,1,0:T(8,128)(2,1)S(1)} %collective-permute-done.12.refs_2_), channel_id=1, source_target_pairs={{0,1},{1,0},{2,3},{3,2},{4,5},{5,4},{6,7},{7,6},{8,9},{9,8},{10,11... | collective-permute-start | bytes 4718600 | tf_op jit(solution)/shard_map/ppermute | solution.py:70
  79.8 13.1 %collective-permute-start.15 = (bf16[3,2,128,1024]{3,2,1,0:T(8,128)(2,1)}, bf16[3,2,128,1024]{3,2,1,0:T(8,128)(2,1)S(1)}, u32[]{:S(2)}, u32[]{:S(2)}) collective-permute-start(bf16[3,2,128,1024]{3,2,1,0:T(8,128)(2,1)} %get-tuple-element.160.refs_0_), channel_id=1, source_target_pairs={{0,1},{1,0},{2,3},{3,2},{4,5},{5,4},{6,7},{7,6},{8,9},{9,8},{10,11... | collective-permute-start | bytes 4718600 | tf_op jit(solution)/shard_map/ppermute | solution.py:70
  80.3 11.6 %collective-permute-start.17 = (bf16[2,256,1024]{2,1,0:T(8,128)(2,1)}, bf16[2,256,1024]{2,1,0:T(8,128)(2,1)S(1)}, u32[]{:S(2)}, u32[]{:S(2)}) collective-permute-start(bf16[2,256,1024]{2,1,0:T(8,128)(2,1)} %collective-permute-done.6.refs_4_), channel_id=1, source_target_pairs={{0,1},{1,0},{2,3},{3,2},{4,5},{5,4},{6,7},{7,6},{8,9},{9,8},{10,11... | collective-permute-start | bytes 3145736 | tf_op jit(solution)/shard_map/ppermute | solution.py:70
  80.3 49.1 %collective-permute-start.14 = (bf16[3,2,128,1024]{3,2,1,0:T(8,128)(2,1)}, bf16[3,2,128,1024]{3,2,1,0:T(8,128)(2,1)S(1)}, u32[]{:S(2)}, u32[]{:S(2)}) collective-permute-start(bf16[3,2,128,1024]{3,2,1,0:T(8,128)(2,1)} %get-tuple-element.165.refs_1_.refs_0_), channel_id=1, source_target_pairs={{0,2},{1,3},{2,0},{3,1},{4,6},{5,7},{6,4},{7,5},{8,10},{9,11},{10,... | collective-permute-start | bytes 4718600 | tf_op jit(solution)/shard_map/ppermute | solution.py:70
  80.9 1.0 copy-start.3
  85.1 44.4 %collective-permute-start.13 = (bf16[6,2,128,256]{3,2,1,0:T(8,128)(2,1)}, bf16[6,2,128,256]{3,2,1,0:T(8,128)(2,1)S(1)}, u32[]{:S(2)}, u32[]{:S(2)}) collective-permute-start(bf16[6,2,128,256]{3,2,1,0:T(8,128)(2,1)} %partial_sums.3), channel_id=1, source_target_pairs={{0,16},{4,20},{8,24},{12,28},{16,0},{20,4},{24,8},{28,12},{1,17},{... | collective-permute-start | bytes 2359304 | tf_op jit(solution)/shard_map/ppermute | solution.py:70
  91.1 0.7 copy-start.11
  91.9 1.0 copy-start.14
  92.8 1.2 copy-start.9
  94.0 35.5 %collective-permute-start.18 = (bf16[3,2,128,256]{3,2,1,0:T(8,128)(2,1)}, bf16[3,2,128,256]{3,2,1,0:T(8,128)(2,1)S(1)}, u32[]{:S(2)}, u32[]{:S(2)}) collective-permute-start(bf16[3,2,128,256]{3,2,1,0:T(8,128)(2,1)} %get-tuple-element.151), channel_id=1, source_target_pairs={{0,4},{4,0},{8,12},{12,8},{16,20},{20,16},{24,28},{28,24},{1,5},{5... | collective-permute-start | bytes 1179656 | tf_op jit(solution)/shard_map/ppermute | solution.py:70
  94.6 34.9 %collective-permute-start.19 = (bf16[3,2,128,256]{3,2,1,0:T(8,128)(2,1)}, bf16[3,2,128,256]{3,2,1,0:T(8,128)(2,1)S(1)}, u32[]{:S(2)}, u32[]{:S(2)}) collective-permute-start(bf16[3,2,128,256]{3,2,1,0:T(8,128)(2,1)} %get-tuple-element.152), channel_id=1, source_target_pairs={{0,8},{4,12},{8,0},{12,4},{16,24},{20,28},{24,16},{28,20},{1,9},{5... | collective-permute-start | bytes 1179656 | tf_op jit(solution)/shard_map/ppermute | solution.py:70
  97.7 34.0 %collective-permute-start.20 = (bf16[3,2,128,256]{3,2,1,0:T(8,128)(2,1)}, bf16[3,2,128,256]{3,2,1,0:T(8,128)(2,1)S(1)}, u32[]{:S(2)}, u32[]{:S(2)}) collective-permute-start(bf16[3,2,128,256]{3,2,1,0:T(8,128)(2,1)} %get-tuple-element.153), channel_id=1, source_target_pairs={{0,12},{4,8},{8,4},{12,0},{16,28},{20,24},{24,20},{28,16},{1,13},{... | collective-permute-start | bytes 1179656 | tf_op jit(solution)/shard_map/ppermute | solution.py:70
  97.7 1.4 copy-start.7
  99.1 1.2 copy-start.15
  100.3 14.8 %copy-start.8 = (bf16[3,2,128,1024]{3,2,1,0:T(8,128)(2,1)S(1)}, bf16[3,2,128,1024]{3,2,1,0:T(8,128)(2,1)}, u32[]{:S(2)}) copy-start(bf16[3,2,128,1024]{3,2,1,0:T(8,128)(2,1)} %get-tuple-element.160.refs_0_) | copy-start | bytes 4718596
  112.4 2.7 %copy-start.2 = (f32[3,2,256,1024]{3,2,1,0:T(8,128)}, f32[3,2,256,1024]{3,2,1,0:T(8,128)S(1)}, u32[]{:S(2)}) copy-start(f32[3,2,256,1024]{3,2,1,0:T(8,128)S(1)} %right_products.1.base) | copy-start | bytes 18874372
  115.1 1.4 copy-start.10
  116.5 15.7 %copy-start.4 = (bf16[3,2,128,256]{3,2,1,0:T(8,128)(2,1)S(1)}, bf16[3,2,128,256]{3,2,1,0:T(8,128)(2,1)}, u32[]{:S(2)}) copy-start(bf16[3,2,128,256]{3,2,1,0:T(8,128)(2,1)} %get-tuple-element.132.refs_0_) | copy-start | bytes 1179652
  126.8 2.7 %copy-start.1 = (f32[3,2,256,1024]{3,2,1,0:T(8,128)}, f32[3,2,256,1024]{3,2,1,0:T(8,128)S(1)}, u32[]{:S(2)}) copy-start(f32[3,2,256,1024]{3,2,1,0:T(8,128)S(1)} %left_products.2.base) | copy-start | bytes 18874372
  129.5 21.1 %copy-start.17 = (bf16[3,2,128,256]{3,2,1,0:T(8,128)(2,1)}, bf16[3,2,128,256]{3,2,1,0:T(8,128)(2,1)S(1)}, u32[]{:S(2)}) copy-start(bf16[3,2,128,256]{3,2,1,0:T(8,128)(2,1)S(1)} %collective-permute-done.18.refs_1_) | copy-start | bytes 1179652
  129.5 21.1 %copy-start.18 = (bf16[3,2,128,256]{3,2,1,0:T(8,128)(2,1)}, bf16[3,2,128,256]{3,2,1,0:T(8,128)(2,1)S(1)}, u32[]{:S(2)}) copy-start(bf16[3,2,128,256]{3,2,1,0:T(8,128)(2,1)S(1)} %collective-permute-done.19.refs_2_) | copy-start | bytes 1179652
  131.7 18.9 %copy-start.19 = (bf16[3,2,128,256]{3,2,1,0:T(8,128)(2,1)}, bf16[3,2,128,256]{3,2,1,0:T(8,128)(2,1)S(1)}, u32[]{:S(2)}) copy-start(bf16[3,2,128,256]{3,2,1,0:T(8,128)(2,1)S(1)} %collective-permute-done.20.refs_3_) | copy-start | bytes 1179652
  131.7 8.6 %collective-permute-start.21 = (bf16[3,2,128,1024]{3,2,1,0:T(8,128)(2,1)S(1)}, bf16[3,2,128,1024]{3,2,1,0:T(8,128)(2,1)S(1)}, u32[]{:S(2)}, u32[]{:S(2)}) collective-permute-start(bf16[3,2,128,1024]{3,2,1,0:T(8,128)(2,1)S(1)} %copy-done.6), channel_id=1, source_target_pairs={{0,1},{1,0},{2,3},{3,2},{4,5},{5,4},{6,7},{7,6},{8,9},{9,8},{10,11... | collective-permute-start | bytes 4718600 | tf_op jit(solution)/shard_map/ppermute | solution.py:70
  131.7 8.6 %collective-permute-start.22 = (bf16[3,2,128,1024]{3,2,1,0:T(8,128)(2,1)S(1)}, bf16[3,2,128,1024]{3,2,1,0:T(8,128)(2,1)S(1)}, u32[]{:S(2)}, u32[]{:S(2)}) collective-permute-start(bf16[3,2,128,1024]{3,2,1,0:T(8,128)(2,1)S(1)} %collective-permute-done.14.refs_2_), channel_id=1, source_target_pairs={{0,1},{1,0},{2,3},{3,2},{4,5},{5,4},{6,7},{7,6},{8,9},{9,8},{10,11... | collective-permute-start | bytes 4718600 | tf_op jit(solution)/shard_map/ppermute | solution.py:70
  136.8 13.8 %copy-start.12 = (bf16[3,2,128,256]{3,2,1,0:T(8,128)(2,1)}, bf16[3,2,128,256]{3,2,1,0:T(8,128)(2,1)S(1)}, u32[]{:S(2)}) copy-start(bf16[3,2,128,256]{3,2,1,0:T(8,128)(2,1)S(1)} %get-tuple-element.168.refs_0_) | copy-start | bytes 1179652
  136.8 23.9 %collective-permute-start.23 = (bf16[3,2,128,256]{3,2,1,0:T(8,128)(2,1)S(1)}, bf16[3,2,128,256]{3,2,1,0:T(8,128)(2,1)S(1)}, u32[]{:S(2)}, u32[]{:S(2)}) collective-permute-start(bf16[3,2,128,256]{3,2,1,0:T(8,128)(2,1)S(1)} %get-tuple-element.169), channel_id=1, source_target_pairs={{0,4},{4,0},{8,12},{12,8},{16,20},{20,16},{24,28},{28,24},{1,5},{5... | collective-permute-start | bytes 1179656 | tf_op jit(solution)/shard_map/ppermute | solution.py:70
  138.2 22.6 %collective-permute-start.24 = (bf16[3,2,128,256]{3,2,1,0:T(8,128)(2,1)S(1)}, bf16[3,2,128,256]{3,2,1,0:T(8,128)(2,1)S(1)}, u32[]{:S(2)}, u32[]{:S(2)}) collective-permute-start(bf16[3,2,128,256]{3,2,1,0:T(8,128)(2,1)S(1)} %get-tuple-element.170), channel_id=1, source_target_pairs={{0,8},{4,12},{8,0},{12,4},{16,24},{20,28},{24,16},{28,20},{1,9},{5... | collective-permute-start | bytes 1179656 | tf_op jit(solution)/shard_map/ppermute | solution.py:70
  138.2 22.5 %collective-permute-start.25 = (bf16[3,2,128,256]{3,2,1,0:T(8,128)(2,1)S(1)}, bf16[3,2,128,256]{3,2,1,0:T(8,128)(2,1)S(1)}, u32[]{:S(2)}, u32[]{:S(2)}) collective-permute-start(bf16[3,2,128,256]{3,2,1,0:T(8,128)(2,1)S(1)} %get-tuple-element.171), channel_id=1, source_target_pairs={{0,12},{4,8},{8,4},{12,0},{16,28},{20,24},{24,20},{28,16},{1,13},{... | collective-permute-start | bytes 1179656 | tf_op jit(solution)/shard_map/ppermute | solution.py:70
  150.6 2.7 %copy-start = (f32[3,2,256,1024]{3,2,1,0:T(8,128)}, f32[3,2,256,1024]{3,2,1,0:T(8,128)S(1)}, u32[]{:S(2)}) copy-start(f32[3,2,256,1024]{3,2,1,0:T(8,128)S(1)} %left_products.3.product) | copy-start | bytes 18874372
  160.7 0.8 copy-start.20
  160.7 0.9 copy-start.21
  160.7 1.0 copy-start.22
